TPU v7x, 512 devices: a whole 4x8x8 slice. The times are simulated.
512 devices in a mesh: span: 8 (over x, core), seq: 64 (over z, y).
Axes of the slice: x: 4, y: 8, z: 8, core: 2. Of those that a mesh axis runs over, the one named last changes fastest.
Arguments:
- latents: bfloat16 [4096, 4096], P(('span', 'seq')), may hold values from -6 to 6
- new_span: bfloat16 [512, 4096], P('seq'), may hold values from -6 to 6
- counts: int32 [9], replicated, may hold values from 128 to 512, as said below
- steps: int32 [2, 8], replicated, may hold values from 0 to 63
- span_mask: int32 [2, 8, 8], replicated, may hold values from 0 to 1, as said below
- q_gain: float32 [64, 4096], replicated, may hold values from -3 to 3
- k_gain: float32 [64, 4096], replicated, may hold values from -3 to 3
- delta: float32 [64], replicated, may hold values from 0.1 to 0.6
Outputs:
- middle: bfloat16 [4096, 4096], P(('span', 'seq'))
- final: bfloat16 [4096, 4096], P(('span', 'seq'))
Inputs may be any that keep to these rules, and one draw needn't show every extreme that they name: `counts`: each span has at least a quarter of its 512 slots live, live slots first; some span has all of them live. `span_mask`: each span sees its own keys; a span never sees a later span's keys; earlier spans are seen or not.
All inputs are finite; a program needn't handle non-finite values.
Results may differ from a plain program's by a relative error of at most 0.0083.
Values may be sent and summed in bfloat16 or wider, within the bound.
No kernel may reach another device: no remote copies, remote signals or barrier semaphores. Data moves between devices by JAX's collectives and lax.ppermute only.
A program may use at most 64 MiB of HBM per device.

v0:
```python
import math

import jax
import jax.numpy as jnp
from jax import lax
from jax.sharding import PartitionSpec as P

HEAD_DIM = 128


def partner(value, axis, distance):
    mask = 2**distance
    pairs = [(source, source ^ mask) for source in range(lax.axis_size(axis))]
    return lax.ppermute(value, axis, pairs)


def shifted(x, axis, by):
    peers = lax.axis_size(axis)
    pairs = [(i, i + by) for i in range(peers) if 0 <= i + by < peers]
    return lax.ppermute(x, axis, pairs)


def norm_heads(block, heads):
    rows = block.shape[0]
    parts = block.astype(jnp.float32).reshape(rows, heads, HEAD_DIM)
    parts = parts * lax.rsqrt(jnp.mean(parts * parts, axis=-1, keepdims=True) + 1e-06)
    return parts.reshape(rows, heads * HEAD_DIM)


def per_device(latents, new_span, counts, steps, span_mask, q_gain, k_gain, delta):
    seq_count = lax.axis_size("seq")
    span_count = lax.axis_size("span")
    width = latents.shape[1]
    heads = width // HEAD_DIM
    split = max(1, seq_count // heads)
    per_dev = heads * split // seq_count
    tok_rows = latents.shape[0]
    half_rows = tok_rows // split
    seq_rank = lax.axis_index("seq")
    span_rank = lax.axis_index("span")
    my_half = seq_rank % split
    scale = 1.0 / math.sqrt(HEAD_DIM)
    received = jnp.arange(seq_count * half_rows, dtype=jnp.int32)
    sender = received // half_rows
    inner = received % half_rows
    own_pos = sender * tok_rows + my_half * half_rows + inner
    key_pos = jnp.concatenate([own_pos, sender * tok_rows + (1 - my_half) * half_rows + inner])

    def to_heads(block):
        shaped = block.reshape(split, half_rows, heads, HEAD_DIM).transpose(2, 0, 1, 3)
        return shaped.reshape(seq_count, per_dev, half_rows, HEAD_DIM)

    def denoise(state, section):
        t_now = steps[section][span_rank]
        counts_now = counts[section : section + span_count]
        mask_row = span_mask[section][span_rank]
        normed = norm_heads(state, heads)
        q_row = lax.dynamic_index_in_dim(q_gain, t_now, 0, keepdims=False)
        k_row = lax.dynamic_index_in_dim(k_gain, t_now, 0, keepdims=False)
        query = (normed * q_row).astype(jnp.bfloat16)
        keyed = (normed * k_row).astype(jnp.bfloat16)
        q_x, k_x, v_x = (
            lax.all_to_all(to_heads(query), "seq", split_axis=0, concat_axis=2, tiled=True),
            lax.all_to_all(to_heads(keyed), "seq", split_axis=0, concat_axis=2, tiled=True),
            lax.all_to_all(to_heads(state), "seq", split_axis=0, concat_axis=2, tiled=True),
        )
        q_x = q_x[0]
        k_x = k_x[0]
        v_x = v_x[0]
        k_other, v_other = partner((k_x, v_x), "seq", 0)
        k_x = jnp.concatenate([k_x, k_other], axis=1)
        v_x = jnp.concatenate([v_x, v_other], axis=1)
        rows_q = q_x.shape[1]
        start_state = (
            jnp.full((per_dev, rows_q), -jnp.inf, jnp.float32),
            jnp.zeros((per_dev, rows_q), jnp.float32),
            jnp.zeros((per_dev, rows_q, HEAD_DIM), jnp.float32),
        )
        carry = start_state
        pieces = (
            lax.all_gather(k_x[None], "span", axis=0, tiled=True),
            lax.all_gather(v_x[None], "span", axis=0, tiled=True),
        )
        start = jnp.int32(0)
        for item in range(pieces[0].shape[0]):
            source = start + item
            allowed = lax.dynamic_index_in_dim(mask_row, source, 0, keepdims=False) > 0
            key_blk = pieces[0][item]
            val_blk = pieces[1][item]
            limit = lax.dynamic_index_in_dim(counts_now, source, 0, keepdims=False)

            def update(state_now):
                top, total, summed = state_now
                score = (
                    jnp.einsum("hqd,hkd->hqk", q_x, key_blk, preferred_element_type=jnp.float32)
                    * scale
                )
                score = jnp.where((key_pos < limit)[None, None, :], score, -jnp.inf)
                top_new = jnp.maximum(top, jnp.max(score, axis=-1))
                factor = jnp.exp(top - top_new)
                weight = jnp.exp(score - top_new[..., None])
                total_new = total * factor + jnp.sum(weight, axis=-1)
                summed_new = summed * factor[..., None] + jnp.einsum(
                    "hqk,hkd->hqd",
                    weight.astype(jnp.bfloat16),
                    val_blk,
                    preferred_element_type=jnp.float32,
                )
                return (top_new, total_new, summed_new)

            carry = lax.cond(allowed, update, lambda kept: kept, carry)
        top, total, summed = carry
        attended = (summed / total[..., None]).astype(jnp.bfloat16)
        returned = lax.all_to_all(attended[None], "seq", split_axis=2, concat_axis=0, tiled=True)
        returned = (
            returned.reshape(heads, split, half_rows, HEAD_DIM)
            .transpose(1, 2, 0, 3)
            .reshape(tok_rows, width)
        )
        rate = lax.dynamic_index_in_dim(delta, t_now, 0, keepdims=False)
        old = state.astype(jnp.float32)
        return (old + rate * (returned.astype(jnp.float32) - old)).astype(jnp.bfloat16)

    middle = denoise(latents, 0)
    moved = shifted(middle, "span", -1)
    entering = jnp.where(span_rank == span_count - 1, new_span, moved)
    final = denoise(entering, 1)
    return (middle, final)


def solution(mesh):
    in_specs = (P(("span", "seq"), None), P("seq", None), P(), P(), P(), P(), P(), P())
    out_specs = (P(("span", "seq"), None), P(("span", "seq"), None))
    return jax.shard_map(
        per_device, mesh=mesh, in_specs=in_specs, out_specs=out_specs, check_vma=False
    )
```

profile of v0, /device:TPU:6, one launch (start us, length us, event | category | flops | bytes accessed | tf_op | source)
XLA Modules:
  0.0 287.9 jit_solution(5177055841765604632)
XLA Ops:
  11.1 0.9 fusion.137
  13.4 1.0 constant_dynamic-slice_fusion
  14.4 1.0 constant_dynamic-slice_fusion.1
  15.7 28.6 %all_to_all.32 = bf16[64,1,4,128]{3,2,1,0:T(4,128)(2,1)S(1)} all-to-all(bf16[64,1,4,128]{3,2,1,0:T(4,128)(2,1)S(1)} %copy.64), channel_id=1, replica_groups=mesh['span'=8,'seq'=64] {'seq'}, dimensions={0} | all-to-all | bytes 131072 | tf_op jit(solution)/shard_map/all_to_all | solution.py:64
  44.3 2.6 collective-permute-start
  46.9 3.5 %collective-permute-done = bf16[1,256,128]{2,1,0:T(8,128)(2,1)S(1)} collective-permute-done((bf16[1,256,128]{2,1,0:T(8,128)(2,1)S(1)}, bf16[1,256,128]{2,1,0:T(8,128)(2,1)S(1)}, u32[]{:S(2)}, u32[]{:S(2)}) %collective-permute-start) | collective-permute-done | bytes 65568 | tf_op jit(solution)/shard_map/ppermute | solution.py:14
  51.2 16.0 %all_to_all.33 = bf16[64,1,4,128]{3,2,1,0:T(4,128)(2,1)S(1)} all-to-all(bf16[64,1,4,128]{3,2,1,0:T(4,128)(2,1)S(1)} %bitcast.512), channel_id=1, replica_groups=mesh['span'=8,'seq'=64] {'seq'}, dimensions={0} | all-to-all | bytes 131072 | tf_op jit(solution)/shard_map/all_to_all | solution.py:65
  67.2 2.6 collective-permute-start.1
  69.8 3.5 %collective-permute-done.1 = bf16[1,256,128]{2,1,0:T(8,128)(2,1)S(1)} collective-permute-done((bf16[1,256,128]{2,1,0:T(8,128)(2,1)S(1)}, bf16[1,256,128]{2,1,0:T(8,128)(2,1)S(1)}, u32[]{:S(2)}, u32[]{:S(2)}) %collective-permute-start.1) | collective-permute-done | bytes 65568 | tf_op jit(solution)/shard_map/ppermute | solution.py:14
  74.8 4.6 %all-to-all-start = ((bf16[64,1,4,128]{3,2,1,0:T(4,128)(2,1)}), bf16[64,1,4,128]{3,2,1,0:T(4,128)(2,1)S(1)}, u32[]{:S(2)}, u32[]{:S(2)}) async-start(bf16[64,1,4,128]{3,2,1,0:T(4,128)(2,1)} %copy.62), calls=%async_computation | async-start | bytes 131072 | tf_op jit(solution)/shard_map/all_to_all | solution.py:63
  86.6 1.3 fusion.180
  87.9 12.9 %all-gather.11.cloned.1.call-done = bf16[8,512,128]{2,1,0:T(8,128)(2,1)} async-done(((bf16[1,512,128]{2,1,0:T(8,128)(2,1)}), bf16[8,512,128]{2,1,0:T(8,128)(2,1)}) %all-gather.11.cloned.1.call-update) | async-done | bytes 1048592 | tf_op jit(solution)/shard_map/all_gather | solution.py:82
  100.8 1.3 fusion.179
  102.7 3.5 %conditional.18 = ((f32[1,256]{1,0:T(1,128)}, f32[1,256]{1,0:T(1,128)S(1)}, f32[1,256,128]{2,1,0:T(8,128)S(1)})) conditional(s32[]{:T(128)} %bitcast.140, (f32[1,256]{1,0:T(1,128)}, f32[1,256]{1,0:T(1,128)S(1)}, f32[1,256,128]{2,1,0:T(8,128)S(1)}) %get-tuple-element.876, (s32[]{:T(128)}, s32[512]{0:T(512)S(1)}, bf16[1,256,128]{2,1,0:T(8,128)(2,1)S(1)}, ...), branch_computations={%region_9.10_spmd, %region_10.13_spmd} | conditional | flops 68092928 | bytes 2182180 | solution.py:111
  106.2 3.5 %conditional.19 = ((f32[1,256]{1,0:T(1,128)}, f32[1,256]{1,0:T(1,128)S(1)}, f32[1,256,128]{2,1,0:T(8,128)S(1)})) conditional(s32[]{:T(128)} %bitcast.139, (f32[1,256]{1,0:T(1,128)}, f32[1,256]{1,0:T(1,128)S(1)}, f32[1,256,128]{2,1,0:T(8,128)S(1)}) %get-tuple-element.877, (s32[]{:T(128)}, s32[512]{0:T(512)S(1)}, ...), branch_computations={%region_13.14_spmd, %region_14.17_spmd} | conditional | flops 68092928 | bytes 2182180 | solution.py:111
  109.7 3.4 %conditional.20 = ((f32[1,256]{1,0:T(1,128)}, f32[1,256]{1,0:T(1,128)S(1)}, f32[1,256,128]{2,1,0:T(8,128)S(1)})) conditional(s32[]{:T(128)} %bitcast.138, (f32[1,256]{1,0:T(1,128)}, f32[1,256]{1,0:T(1,128)S(1)}, f32[1,256,128]{2,1,0:T(8,128)S(1)}) %get-tuple-element.878, (s32[]{:T(128)}, s32[512]{0:T(512)S(1)}, ...), branch_computations={%region_17.18_spmd, %region_18.21_spmd} | conditional | flops 68092928 | bytes 2182180 | solution.py:111
  113.1 5.2 %conditional.22 = ((f32[1,256]{1,0:T(1,128)}, f32[1,256]{1,0:T(1,128)S(1)}, f32[1,256,128]{2,1,0:T(8,128)S(1)})) conditional(s32[]{:T(128)} %bitcast.136, (f32[1,256]{1,0:T(1,128)}, f32[1,256]{1,0:T(1,128)S(1)}, f32[1,256,128]{2,1,0:T(8,128)S(1)}) %get-tuple-element.880, (s32[]{:T(128)}, s32[512]{0:T(512)S(1)}, ...), branch_computations={%region_25.26_spmd, %region_26.29_spmd} | conditional | flops 68092928 | bytes 2182180 | solution.py:111
  113.7 1.2 fusion.168
  116.6 1.2 fusion.55
  119.1 1.0 reduce.64
  120.8 13.0 %all-to-all-start.3 = ((bf16[64,2,256]{2,1,0:T(2,128)(2,1)}), bf16[64,2,256]{2,1,0:T(2,128)(2,1)S(1)}, u32[]{:S(2)}, u32[]{:S(2)}) async-start(bf16[64,2,256]{2,1,0:T(2,128)(2,1)} %reshape.840), calls=%async_computation.3 | async-start | bytes 131072 | tf_op jit(solution)/shard_map/all_to_all | solution.py:114
  134.4 11.6 %all-to-all-done.3 = bf16[64,2,256]{2,1,0:T(2,128)(2,1)S(1)} async-done(((bf16[64,2,256]{2,1,0:T(2,128)(2,1)}), bf16[64,2,256]{2,1,0:T(2,128)(2,1)S(1)}, u32[]{:S(2)}, u32[]{:S(2)}) %all-to-all-start.3) | async-done | bytes 65568 | tf_op jit(solution)/shard_map/all_to_all | solution.py:114
  146.9 3.9 %collective-permute-start.2 = (bf16[8,4096]{1,0:T(8,128)(2,1)S(1)}, bf16[8,4096]{1,0:T(8,128)(2,1)S(1)}, u32[]{:S(2)}, u32[]{:S(2)}) collective-permute-start(bf16[8,4096]{1,0:T(8,128)(2,1)S(1)} %fusion.139), channel_id=1, source_target_pairs={{64,0},{128,64},{192,128},{256,192},{320,256},{384,320},{448,384},... | collective-permute-start | bytes 196616 | tf_op jit(solution)/shard_map/ppermute | solution.py:20
  150.8 1.9 collective-permute-done.2
  153.1 16.1 %all_to_all.34 = bf16[64,1,4,128]{3,2,1,0:T(4,128)(2,1)S(1)} all-to-all(bf16[64,1,4,128]{3,2,1,0:T(4,128)(2,1)S(1)} %copy.75), channel_id=1, replica_groups=mesh['span'=8,'seq'=64] {'seq'}, dimensions={0} | all-to-all | bytes 131072 | tf_op jit(solution)/shard_map/all_to_all | solution.py:64
  169.1 2.6 collective-permute-start.3
  171.7 3.6 %collective-permute-done.3 = bf16[1,256,128]{2,1,0:T(8,128)(2,1)S(1)} collective-permute-done((bf16[1,256,128]{2,1,0:T(8,128)(2,1)S(1)}, bf16[1,256,128]{2,1,0:T(8,128)(2,1)S(1)}, u32[]{:S(2)}, u32[]{:S(2)}) %collective-permute-start.3) | collective-permute-done | bytes 65568 | tf_op jit(solution)/shard_map/ppermute | solution.py:14
  176.2 16.0 %all_to_all.35 = bf16[64,1,4,128]{3,2,1,0:T(4,128)(2,1)S(1)} all-to-all(bf16[64,1,4,128]{3,2,1,0:T(4,128)(2,1)S(1)} %copy.77), channel_id=1, replica_groups=mesh['span'=8,'seq'=64] {'seq'}, dimensions={0} | all-to-all | bytes 131072 | tf_op jit(solution)/shard_map/all_to_all | solution.py:65
  192.2 2.6 collective-permute-start.4
  194.8 3.5 %collective-permute-done.4 = bf16[1,256,128]{2,1,0:T(8,128)(2,1)S(1)} collective-permute-done((bf16[1,256,128]{2,1,0:T(8,128)(2,1)S(1)}, bf16[1,256,128]{2,1,0:T(8,128)(2,1)S(1)}, u32[]{:S(2)}, u32[]{:S(2)}) %collective-permute-start.4) | collective-permute-done | bytes 65568 | tf_op jit(solution)/shard_map/ppermute | solution.py:14
  205.6 4.6 %all-to-all-start.4 = ((bf16[64,1,4,128]{3,2,1,0:T(4,128)(2,1)}), bf16[64,1,4,128]{3,2,1,0:T(4,128)(2,1)S(1)}, u32[]{:S(2)}, u32[]{:S(2)}) async-start(bf16[64,1,4,128]{3,2,1,0:T(4,128)(2,1)} %copy.73), calls=%async_computation.4 | async-start | bytes 131072 | tf_op jit(solution)/shard_map/all_to_all | solution.py:63
  210.2 1.3 fusion.178
  211.5 13.7 %all-gather.15.cloned.1.call-done = bf16[8,512,128]{2,1,0:T(8,128)(2,1)} async-done(((bf16[1,512,128]{2,1,0:T(8,128)(2,1)}), bf16[8,512,128]{2,1,0:T(8,128)(2,1)}) %all-gather.15.cloned.1.call-update) | async-done | bytes 1048592 | tf_op jit(solution)/shard_map/all_gather | solution.py:82
  225.2 1.3 fusion.177
  226.5 4.8 %conditional.24 = (f32[1,256]{1,0:T(1,128)}, f32[1,256]{1,0:T(1,128)S(1)}, f32[1,256,128]{2,1,0:T(8,128)S(1)}) conditional(s32[]{:T(128)} %bitcast.181, () %tuple.120, (s32[]{:T(128)}, s32[512]{0:T(512)S(1)}, bf16[1,256,128]{2,1,0:T(8,128)(2,1)S(1)}, bf16[1,512,128]{2,1,0:T(8,128)(2,1)S(1)}, bf16[1,512,128]{2,1,0:T(8,128)(2,1)S(1)}) %tuple.301), branch_computations={%region_34.35_spmd, %region_35.38_spmd} | conditional | flops 68060416 | bytes 2044956 | solution.py:111
  228.0 0.9 fusion.71
  230.3 1.0 fusion.69
  231.3 3.5 %conditional.25 = ((f32[1,256]{1,0:T(1,128)}, f32[1,256]{1,0:T(1,128)S(1)}, f32[1,256,128]{2,1,0:T(8,128)S(1)})) conditional(s32[]{:T(128)} %bitcast.180, (f32[1,256]{1,0:T(1,128)}, f32[1,256]{1,0:T(1,128)S(1)}, f32[1,256,128]{2,1,0:T(8,128)S(1)}) %conditional.24, (s32[]{:T(128)}, s32[512]{0:T(512)S(1)}, bf16[1,256,128]{2,1,0:T(8,128)(2,1)S(1)}, ...), branch_computations={%region_38.39_spmd, %region_39.42_spmd} | conditional | flops 68092928 | bytes 2182180 | solution.py:111
  234.7 3.5 %conditional.26 = ((f32[1,256]{1,0:T(1,128)}, f32[1,256]{1,0:T(1,128)S(1)}, f32[1,256,128]{2,1,0:T(8,128)S(1)})) conditional(s32[]{:T(128)} %bitcast.179, (f32[1,256]{1,0:T(1,128)}, f32[1,256]{1,0:T(1,128)S(1)}, f32[1,256,128]{2,1,0:T(8,128)S(1)}) %get-tuple-element.883, (s32[]{:T(128)}, s32[512]{0:T(512)S(1)}, ...), branch_computations={%region_42.43_spmd, %region_43.46_spmd} | conditional | flops 68092928 | bytes 2182180 | solution.py:111
  238.3 3.4 %conditional.27 = ((f32[1,256]{1,0:T(1,128)}, f32[1,256]{1,0:T(1,128)S(1)}, f32[1,256,128]{2,1,0:T(8,128)S(1)})) conditional(s32[]{:T(128)} %bitcast.178, (f32[1,256]{1,0:T(1,128)}, f32[1,256]{1,0:T(1,128)S(1)}, f32[1,256,128]{2,1,0:T(8,128)S(1)}) %get-tuple-element.884, (s32[]{:T(128)}, s32[512]{0:T(512)S(1)}, ...), branch_computations={%region_46.47_spmd, %region_47.50_spmd} | conditional | flops 68092928 | bytes 2182180 | solution.py:111
  241.7 3.4 %conditional.28 = ((f32[1,256]{1,0:T(1,128)}, f32[1,256]{1,0:T(1,128)S(1)}, f32[1,256,128]{2,1,0:T(8,128)S(1)})) conditional(s32[]{:T(128)} %bitcast.177, (f32[1,256]{1,0:T(1,128)}, f32[1,256]{1,0:T(1,128)S(1)}, f32[1,256,128]{2,1,0:T(8,128)S(1)}) %get-tuple-element.885, (s32[]{:T(128)}, s32[512]{0:T(512)S(1)}, ...), branch_computations={%region_50.51_spmd, %region_51.54_spmd} | conditional | flops 68092928 | bytes 2182180 | solution.py:111
  245.1 3.4 %conditional.29 = ((f32[1,256]{1,0:T(1,128)}, f32[1,256]{1,0:T(1,128)S(1)}, f32[1,256,128]{2,1,0:T(8,128)S(1)})) conditional(s32[]{:T(128)} %bitcast.176, (f32[1,256]{1,0:T(1,128)}, f32[1,256]{1,0:T(1,128)S(1)}, f32[1,256,128]{2,1,0:T(8,128)S(1)}) %get-tuple-element.886, (s32[]{:T(128)}, s32[512]{0:T(512)S(1)}, ...), branch_computations={%region_54.55_spmd, %region_55.58_spmd} | conditional | flops 68092928 | bytes 2182180 | solution.py:111
  248.6 5.2 %conditional.30 = ((f32[1,256]{1,0:T(1,128)}, f32[1,256]{1,0:T(1,128)S(1)}, f32[1,256,128]{2,1,0:T(8,128)S(1)})) conditional(s32[]{:T(128)} %bitcast.175, (f32[1,256]{1,0:T(1,128)}, f32[1,256]{1,0:T(1,128)S(1)}, f32[1,256,128]{2,1,0:T(8,128)S(1)}) %get-tuple-element.887, (s32[]{:T(128)}, s32[512]{0:T(512)S(1)}, ...), branch_computations={%region_58.59_spmd, %region_59.62_spmd} | conditional | flops 68092928 | bytes 2182180 | solution.py:111
  249.1 1.2 fusion.175
  252.0 1.2 fusion.123
  254.0 1.0 reduce.65
  255.0 24.9 %all_to_all.36 = bf16[64,2,256]{2,1,0:T(2,128)(2,1)S(1)} all-to-all(bf16[64,2,256]{2,1,0:T(2,128)(2,1)S(1)} %reshape.842), channel_id=1, replica_groups=mesh['span'=8,'seq'=64] {'seq'}, dimensions={0} | all-to-all | bytes 131072 | tf_op jit(solution)/shard_map/all_to_all | solution.py:114
  280.1 1.3 fusion.143
  (150 shorter events, 49.7 us)
Async XLA Ops:
  7.2 79.5 %all-gather.9.cloned.1.call-start = ((), (), s32[]{:S(2)}) async-start(), calls=%async_computation.8 | async-start | bytes 1179648 | tf_op jit(solution)/shard_map/all_gather | solution.py:81
  7.2 0.7 copy-start.6
  13.3 2.1 copy-start
  44.3 6.1 %collective-permute-start = (bf16[1,256,128]{2,1,0:T(8,128)(2,1)S(1)}, bf16[1,256,128]{2,1,0:T(8,128)(2,1)S(1)}, u32[]{:S(2)}, u32[]{:S(2)}) collective-permute-start(bf16[1,256,128]{2,1,0:T(8,128)(2,1)S(1)} %bitcast.528), channel_id=1, source_target_pairs={{0,1},{1,0},{2,3},{3,2},{4,5},{5,4},{6,7},{7,6},{8,9},{9,8},{10,11... | collective-permute-start | bytes 196616 | tf_op jit(solution)/shard_map/ppermute | solution.py:14
  51.1 49.7 %all-gather.11.cloned.1.call-start = ((), (), s32[]{:S(2)}) async-start(), calls=%async_computation.9 | async-start | bytes 1179648 | tf_op jit(solution)/shard_map/all_gather | solution.py:82
  67.2 6.1 %collective-permute-start.1 = (bf16[1,256,128]{2,1,0:T(8,128)(2,1)S(1)}, bf16[1,256,128]{2,1,0:T(8,128)(2,1)S(1)}, u32[]{:S(2)}, u32[]{:S(2)}) collective-permute-start(bf16[1,256,128]{2,1,0:T(8,128)(2,1)S(1)} %bitcast.534), channel_id=1, source_target_pairs={{0,1},{1,0},{2,3},{3,2},{4,5},{5,4},{6,7},{7,6},{8,9},{9,8},{10,11... | collective-permute-start | bytes 196616 | tf_op jit(solution)/shard_map/ppermute | solution.py:14
  74.8 27.3 %all-to-all-start = ((bf16[64,1,4,128]{3,2,1,0:T(4,128)(2,1)}), bf16[64,1,4,128]{3,2,1,0:T(4,128)(2,1)S(1)}, u32[]{:S(2)}, u32[]{:S(2)}) async-start(bf16[64,1,4,128]{3,2,1,0:T(4,128)(2,1)} %copy.62), calls=%async_computation | async-start | bytes 131072 | tf_op jit(solution)/shard_map/all_to_all | solution.py:63
  79.4 0.7 copy-start.4
  84.0 1.9 copy-start.3
  120.8 13.0 %copy-start.5 = (f32[64]{0:T(128)S(1)}, f32[64]{0:T(128)}, u32[]{:S(2)}) copy-start(f32[64]{0:T(128)} %param.47) | copy-start | bytes 772
  120.8 25.2 %all-to-all-start.3 = ((bf16[64,2,256]{2,1,0:T(2,128)(2,1)}), bf16[64,2,256]{2,1,0:T(2,128)(2,1)S(1)}, u32[]{:S(2)}, u32[]{:S(2)}) async-start(bf16[64,2,256]{2,1,0:T(2,128)(2,1)} %reshape.840), calls=%async_computation.3 | async-start | bytes 131072 | tf_op jit(solution)/shard_map/all_to_all | solution.py:114
  133.8 76.5 %all-gather.13.cloned.1.call-start = ((), (), s32[]{:S(2)}) async-start(), calls=%async_computation.10 | async-start | bytes 1179648 | tf_op jit(solution)/shard_map/all_gather | solution.py:81
  146.2 6.5 %copy-start.1 = (bf16[8,4096]{1,0:T(8,128)(2,1)S(1)}, bf16[8,4096]{1,0:T(8,128)(2,1)}, u32[]{:S(2)}) copy-start(bf16[8,4096]{1,0:T(8,128)(2,1)} %param.41) | copy-start | bytes 196612
  146.9 5.9 %copy-start.2 = (bf16[8,4096]{1,0:T(8,128)(2,1)}, bf16[8,4096]{1,0:T(8,128)(2,1)S(1)}, u32[]{:S(2)}) copy-start(bf16[8,4096]{1,0:T(8,128)(2,1)S(1)} %fusion.139) | copy-start | bytes 196612
  146.9 5.8 %collective-permute-start.2 = (bf16[8,4096]{1,0:T(8,128)(2,1)S(1)}, bf16[8,4096]{1,0:T(8,128)(2,1)S(1)}, u32[]{:S(2)}, u32[]{:S(2)}) collective-permute-start(bf16[8,4096]{1,0:T(8,128)(2,1)S(1)} %fusion.139), channel_id=1, source_target_pairs={{64,0},{128,64},{192,128},{256,192},{320,256},{384,320},{448,384},... | collective-permute-start | bytes 196616 | tf_op jit(solution)/shard_map/ppermute | solution.py:20
  169.1 6.1 %collective-permute-start.3 = (bf16[1,256,128]{2,1,0:T(8,128)(2,1)S(1)}, bf16[1,256,128]{2,1,0:T(8,128)(2,1)S(1)}, u32[]{:S(2)}, u32[]{:S(2)}) collective-permute-start(bf16[1,256,128]{2,1,0:T(8,128)(2,1)S(1)} %bitcast.530), channel_id=1, source_target_pairs={{0,1},{1,0},{2,3},{3,2},{4,5},{5,4},{6,7},{7,6},{8,9},{9,8},{10,11... | collective-permute-start | bytes 196616 | tf_op jit(solution)/shard_map/ppermute | solution.py:14
  176.0 49.2 %all-gather.15.cloned.1.call-start = ((), (), s32[]{:S(2)}) async-start(), calls=%async_computation.11 | async-start | bytes 1179648 | tf_op jit(solution)/shard_map/all_gather | solution.py:82
  192.2 6.1 %collective-permute-start.4 = (bf16[1,256,128]{2,1,0:T(8,128)(2,1)S(1)}, bf16[1,256,128]{2,1,0:T(8,128)(2,1)S(1)}, u32[]{:S(2)}, u32[]{:S(2)}) collective-permute-start(bf16[1,256,128]{2,1,0:T(8,128)(2,1)S(1)} %bitcast.532), channel_id=1, source_target_pairs={{0,1},{1,0},{2,3},{3,2},{4,5},{5,4},{6,7},{7,6},{8,9},{9,8},{10,11... | collective-permute-start | bytes 196616 | tf_op jit(solution)/shard_map/ppermute | solution.py:14
  205.6 20.9 %all-to-all-start.4 = ((bf16[64,1,4,128]{3,2,1,0:T(4,128)(2,1)}), bf16[64,1,4,128]{3,2,1,0:T(4,128)(2,1)S(1)}, u32[]{:S(2)}, u32[]{:S(2)}) async-start(bf16[64,1,4,128]{3,2,1,0:T(4,128)(2,1)} %copy.73), calls=%async_computation.4 | async-start | bytes 131072 | tf_op jit(solution)/shard_map/all_to_all | solution.py:63
Sparse Core Ops, SparseCore 0:
  51.2 18.7 all-gather.8
  74.1 26.6 all-gather.10
  176.1 18.4 all-gather.12
  199.2 26.0 all-gather.14
where the time goes:
time: 290 us; the launch traced here: 288 us
  blocking collectives  102 us (35%)
  waiting for transfers between devices  54.3 us (19%)
  starting transfers between devices  36.7 us (13%)
  other arithmetic  33.7 us (12%)
  between operations  28.3 us (10%)
  local copies, waits for them, and re-layouts  21.4 us (7%)
  matrix products  11.7 us (4%)
    all_to_all x2, blocking collectives, denoise(): lax.all_to_all(to_heads(keyed), 'seq', split_axis=0, concat_axis=2, tiled...  44.7 us
    all_to_all x2, blocking collectives, denoise(): lax.all_to_all(to_heads(state), 'seq', split_axis=0, concat_axis=2, tiled...  32 us
    all_gather x2, waiting for transfers between devices, denoise(): lax.all_gather(v_x[None], 'span', axis=0, tiled=True)  26.6 us
    all_to_all x1, blocking collectives, denoise(): lax.all_to_all(attended[None], 'seq', split_axis=2, concat_axis=0, tiled=...  24.9 us
    ppermute x4, waiting for transfers between devices, partner(): return lax.ppermute(value, axis, pairs)  14.1 us
    all_to_all x1, starting transfers between devices, denoise(): lax.all_to_all(attended[None], 'seq', split_axis=2, concat_axis=0, tiled=...  13 us
    all_to_all x1, waiting for transfers between devices, denoise(): lax.all_to_all(attended[None], 'seq', split_axis=2, concat_axis=0, tiled=...  11.6 us
    ppermute x4, starting transfers between devices, partner(): return lax.ppermute(value, axis, pairs)  10.5 us
  transfers between devices with their start and end apart: 12, of which 8 were waited for; matrix products, arithmetic and copies ran while one was open for 4% of the time, Pallas kernels for 0%

commit v1 on v0

v1 whole, which is shorter than its diff:
```python
import functools
import math

import jax
import jax.numpy as jnp
from jax import lax
from jax.experimental import pallas as pl
from jax.experimental.pallas import tpu as pltpu
from jax.sharding import Mesh
from jax.sharding import PartitionSpec as P

HEAD_DIM = 128
SPAN = 512
SPANS = 8
HALF = SPAN // 2
SCORE_SCALE = math.log2(math.e) / math.sqrt(HEAD_DIM)
SHIFT = 40.0
SMALL = 2.0**-60


def normed(x):
    x = x.astype(jnp.float32)
    return x * lax.rsqrt(jnp.mean(x * x, axis=-1, keepdims=True) + 1e-06)


def head_kernel(
    place,
    counts,
    steps,
    mask,
    delta,
    q_gain,
    k_gain,
    same,
    other,
    fresh,
    out,
    qg,
    kg,
    xs,
    query,
    key,
    value,
    query2,
    key2,
    value2,
    acc,
    low,
    sems,
):
    g, half, head, core = place()
    cols = pl.ds(pl.multiple_of(head * HEAD_DIM, HEAD_DIM), HEAD_DIM)
    copies = [
        pltpu.make_async_copy(q_gain.at[:, cols], qg, sems.at[0]),
        pltpu.make_async_copy(k_gain.at[:, cols], kg, sems.at[1]),
    ]
    for copy in copies:
        copy.start()
    for copy in copies:
        copy.wait()

    slot = lax.broadcasted_iota(jnp.int32, (SPAN, HEAD_DIM), 0)

    def make_key(x, t, live, i, key, value):
        n = normed(x)
        key[i] = (n * kg[pl.ds(t, 1), :]).T.astype(jnp.bfloat16)
        alive = slot < live
        value[i, :, :HEAD_DIM] = jnp.where(alive, x.astype(jnp.float32), 0.0).astype(jnp.bfloat16)
        value[i, :, HEAD_DIM:] = jnp.where(alive, 1.0, 0.0).astype(jnp.bfloat16)
        return n

    def make_query(n, t):
        return (n * qg[pl.ds(t, 1), :]).astype(jnp.bfloat16)

    last = jnp.minimum(g + half, SPANS - 1)
    for a in range(SPANS // 2):
        for source, j in ((same, 2 * a + core), (other, 2 * a + 1 - core)):

            @pl.when(j <= last)
            def _():
                x = source[a]
                xs[j] = x
                t = steps[0, j]
                n = make_key(x, t, counts[j], j, key, value)
                query[j] = make_query(n, t)

    def attend(q, rows, key, value, row_mask, live, upto, safe):
        acc[:rows] = jnp.zeros((rows, 2 * HEAD_DIM), jnp.float32)
        if safe:
            low[:rows] = jnp.full((rows, HEAD_DIM), -1e30, jnp.float32)

        def scores(i, width):
            s = jnp.dot(q, key[i, :, :width], preferred_element_type=jnp.float32) * SCORE_SCALE
            if not safe:
                return s
            at = lax.broadcasted_iota(jnp.int32, (rows, width), 1)
            return jnp.where(at < live(i), s, -1e30)

        def over_spans(step):
            def one(i, carry):
                @pl.when(row_mask(i) > 0)
                def _():
                    @pl.when(live(i) > HALF)
                    def _():
                        step(i, SPAN)

                    @pl.when(live(i) <= HALF)
                    def _():
                        step(i, HALF)

                return carry

            lax.fori_loop(0, upto, one, 0)

        def highest(i, width):
            top = jnp.max(scores(i, width), axis=-1, keepdims=True)
            low[:rows] = jnp.maximum(low[:rows], top)

        def add(i, width):
            shift = low[:rows, :1] if safe else SHIFT
            weight = jnp.exp2(scores(i, width) - shift).astype(jnp.bfloat16)
            acc[:rows] += jnp.dot(weight, value[i, :width], preferred_element_type=jnp.float32)

        if safe:
            over_spans(highest)
        over_spans(add)

    def finish(x, rows, rate):
        total = acc[:rows, HEAD_DIM:]
        attended = (acc[:rows, :HEAD_DIM] / total).astype(jnp.bfloat16).astype(jnp.float32)
        old = x.astype(jnp.float32)
        return (old + rate * (attended - old)).astype(jnp.bfloat16), jnp.min(total)

    def first_step(safe):
        def one(j, worst):
            whole = jnp.logical_or(half == 0, j == g + 1)
            needed = jnp.where(half == 0, j == g, jnp.logical_and(j >= 1, mask[1, g, jnp.maximum(j - 1, 0)] > 0))
            t = steps[0, j]
            live = lambda i: counts[i]

            def block(rows):
                attend(query[j, :rows], rows, key, value, lambda i: mask[0, j, i], live, j + 1, safe)
                x, least = finish(xs[j, :rows], rows, delta[t])

                @pl.when(half == 0)
                def _():
                    out[:rows] = x

                @pl.when(half == 1)
                def _():
                    e = j - 1
                    n = normed(x)
                    t2 = steps[1, e]
                    key2[e, :, :rows] = (n * kg[pl.ds(t2, 1), :]).T.astype(jnp.bfloat16)
                    alive = slot[:rows] < counts[j]
                    value2[e, :rows, :HEAD_DIM] = jnp.where(alive, x.astype(jnp.float32), 0.0).astype(jnp.bfloat16)
                    value2[e, :rows, HEAD_DIM:] = jnp.where(alive, 1.0, 0.0).astype(jnp.bfloat16)

                    @pl.when(e == g)
                    def _():
                        xs[SPANS, :rows] = x
                        query2[:rows] = make_query(n, t2)

                return least

            def run():
                return lax.cond(
                    jnp.logical_or(whole, counts[j] > HALF), lambda: block(SPAN), lambda: block(HALF)
                )

            return jnp.minimum(worst, lax.cond(needed, run, lambda: jnp.float32(1.0)))

        return lax.fori_loop(0, last + 1, one, jnp.float32(1.0))

    @pl.when(first_step(False) < SMALL)
    def _():
        first_step(True)

    def second_step(safe):
        attend(query2[...], SPAN, key2, value2, lambda e: mask[1, g, e], lambda e: counts[e + 1], g + 1, safe)
        x, least = finish(xs[SPANS], SPAN, delta[steps[1, g]])
        out[...] = x
        return least

    @pl.when(half == 1)
    def _():
        @pl.when(g == SPANS - 1)
        def _():
            x = fresh[...]
            xs[SPANS] = x
            t2 = steps[1, g]
            n = make_key(x, t2, counts[SPANS], SPANS - 1, key2, value2)
            query2[...] = make_query(n, t2)

        @pl.when(second_step(False) < SMALL)
        def _():
            second_step(True)


def mesh_place():
    seq = lax.axis_index("seq")
    core = lax.axis_index("core")
    return 2 * lax.axis_index("x") + core, lax.rem(seq, 2), seq // 2, core


def both_steps(place, counts, steps, mask, delta, q_gain, k_gain, same, other, fresh, interpret=False):
    smem = pl.BlockSpec(memory_space=pltpu.SMEM)
    hbm = pl.BlockSpec(memory_space=pl.ANY)
    vmem = pl.BlockSpec(memory_space=pltpu.VMEM)
    noise_steps = q_gain.shape[0]
    bf16, f32 = jnp.bfloat16, jnp.float32
    return pl.pallas_call(
        functools.partial(head_kernel, place),
        out_shape=jax.ShapeDtypeStruct((SPAN, HEAD_DIM), bf16),
        in_specs=[smem, smem, smem, smem, hbm, hbm, vmem, vmem, vmem],
        out_specs=vmem,
        scratch_shapes=[
            pltpu.VMEM((noise_steps, HEAD_DIM), f32),
            pltpu.VMEM((noise_steps, HEAD_DIM), f32),
            pltpu.VMEM((SPANS + 1, SPAN, HEAD_DIM), bf16),
            pltpu.VMEM((SPANS, SPAN, HEAD_DIM), bf16),
            pltpu.VMEM((SPANS, HEAD_DIM, SPAN), bf16),
            pltpu.VMEM((SPANS, SPAN, 2 * HEAD_DIM), bf16),
            pltpu.VMEM((SPAN, HEAD_DIM), bf16),
            pltpu.VMEM((SPANS, HEAD_DIM, SPAN), bf16),
            pltpu.VMEM((SPANS, SPAN, 2 * HEAD_DIM), bf16),
            pltpu.VMEM((SPAN, 2 * HEAD_DIM), f32),
            pltpu.VMEM((SPAN, HEAD_DIM), f32),
            pltpu.SemaphoreType.DMA((2,)),
        ],
        compiler_params=pltpu.CompilerParams(vmem_limit_bytes=32 * 1024 * 1024),
        interpret=interpret,
    )(counts, steps, mask, delta, q_gain, k_gain, same, other, fresh)


def per_device(latents, new_span, counts, steps, span_mask, q_gain, k_gain, delta):
    rows, width = latents.shape
    heads = width // HEAD_DIM

    def to_heads(block):
        return block.reshape(rows, heads, HEAD_DIM).transpose(1, 0, 2)

    sent = jnp.concatenate([to_heads(latents), to_heads(new_span)], axis=1)
    sent = jnp.broadcast_to(sent[:, None], (heads, 2, 2 * rows, HEAD_DIM)).reshape(2 * heads, 2 * rows, HEAD_DIM)
    got = lax.all_to_all(sent, "seq", 0, 0, tiled=True)
    mine = got[:, :rows].reshape(SPAN, HEAD_DIM)
    fresh = got[:, rows:].reshape(SPAN, HEAD_DIM)
    same = lax.all_gather(mine, "x", axis=0)
    other = lax.ppermute(same, "core", [(0, 1), (1, 0)])
    done = both_steps(mesh_place, counts, steps, span_mask, delta, q_gain, k_gain, same, other, fresh)
    back = lax.all_to_all(done.reshape(2 * heads, rows, HEAD_DIM), "seq", 0, 0, tiled=True)
    back = back.reshape(heads, 2, rows, HEAD_DIM)
    return tuple(back[:, k].transpose(1, 0, 2).reshape(rows, width) for k in range(2))


def solution(mesh):
    mesh = Mesh(mesh.devices.reshape(4, 2, 64), ("x", "core", "seq"))
    tokens = P(("x", "core", "seq"), None)
    in_specs = (tokens, P("seq", None), P(), P(), P(), P(), P(), P())
    return jax.shard_map(per_device, mesh=mesh, in_specs=in_specs, out_specs=(tokens, tokens), check_vma=False)
```

time: 290 us -> 84.6 us (0.29)
  waiting for transfers between devices: 54.3 us -> 1.88 us
  starting transfers between devices: 36.7 us -> 2.04 us
  other arithmetic: 33.7 us -> 0.9 us
  blocking collectives: 102 us -> 72.5 us
  between operations: 28.3 us -> 0.72 us
  local copies, waits for them, and re-layouts: 21.4 us -> 0.75 us
  matrix products: 11.7 us -> 0 us
  Pallas kernels: 0 us -> 4.73 us
    all_to_all x5 -> x2, blocking collectives: 102 us -> 59.7 us  [the longest x1 31.4 us: per_device(): got = lax.all_to_all(sent, 'seq', 0, 0, tiled=True)]
    all_gather x4 -> x0, waiting for transfers between devices: 26.6 us -> none  [the longest x2 26.6 us: denoise(): lax.all_gather(v_x[None], 'span', axis=0, tiled=True)]
    all_to_all x3 -> x0, starting transfers between devices: 22.2 us -> none  [the longest x1 13 us: denoise(): lax.all_to_all(attended[None], 'seq', split_axis=2, concat_axis=0, tiled=...]
    ppermute x5 -> x1, waiting for transfers between devices: 16 us -> 1.88 us  [per_device(): other = lax.ppermute(same, 'core', [(0, 1), (1, 0)])]
    all_gather x0 -> x1, blocking collectives: none -> 12.8 us  [per_device(): same = lax.all_gather(mine, 'x', axis=0)]
    ppermute x5 -> x1, starting transfers between devices: 14.3 us -> 2.04 us  [per_device(): other = lax.ppermute(same, 'core', [(0, 1), (1, 0)])]
    dot_general x22 -> x0, matrix products: 11.7 us -> none  [the longest x11 5.87 us: update(): jnp.einsum('hqk,hkd->hqd', weight.astype(jnp.bfloat16), val_blk, preferre...]
    all_to_all x3 -> x0, waiting for transfers between devices: 11.6 us -> none  [the longest x1 11.6 us: denoise(): lax.all_to_all(attended[None], 'seq', split_axis=2, concat_axis=0, tiled=...]
  transfers between devices with their start and end apart: 12 -> 1, of which waited for: 8 -> 1; matrix products, arithmetic and copies ran while one was open for 4% -> 0% of each run, Pallas kernels for 0% -> 0%
where the time goes in v1:
time: 84.6 us; the launch traced here: 83.5 us
  blocking collectives  72.5 us (86%)
  Pallas kernels  4.73 us (6%)
  starting transfers between devices  2.04 us (2%)
  waiting for transfers between devices  1.88 us (2%)
  other arithmetic  0.9 us (1%)
    all_to_all x1, blocking collectives, per_device(): got = lax.all_to_all(sent, 'seq', 0, 0, tiled=True)  31.4 us
    all_to_all x1, blocking collectives, per_device(): lax.all_to_all(done.reshape(2 * heads, rows, HEAD_DIM), 'seq', 0, 0, tile...  28.3 us
    all_gather x1, blocking collectives, per_device(): same = lax.all_gather(mine, 'x', axis=0)  12.8 us
    pallas_call x1, Pallas kernels, both_steps(): pl.pallas_call(functools.partial(head_kernel, place), out_shape=jax.Shape...  4.73 us
    ppermute x1, starting transfers between devices, per_device(): other = lax.ppermute(same, 'core', [(0, 1), (1, 0)])  2.04 us
    ppermute x1, waiting for transfers between devices, per_device(): other = lax.ppermute(same, 'core', [(0, 1), (1, 0)])  1.88 us
  transfers between devices with their start and end apart: 1, of which 1 were waited for; matrix products, arithmetic and copies ran while one was open for 0% of the time, Pallas kernels for 0%

profile of v1, /device:TPU:6, one launch (start us, length us, event | category | flops | bytes accessed | tf_op | source)
XLA Modules:
  0.0 83.5 jit_solution(17155758549860049961)
XLA Ops:
  0.6 0.0 copy-start.2
  0.6 0.9 %pad_maximum_fusion = bf16[32,16,128]{2,1,0:T(8,128)(2,1)S(1)} fusion(bf16[32,8,128]{2,1,0:T(8,128)(2,1)} %bitcast.32, bf16[32,8,128]{2,1,0:T(8,128)(2,1)} %bitcast.33), kind=kLoop, calls=%fused_computation.2 | loop fusion | flops 262144 | bytes 262144 | tf_op jit(solution)/shard_map/concatenate | solution.py:243
  1.5 0.0 copy-start
  1.6 0.0 copy-start.1
  1.6 31.4 %all_to_all.10 = bf16[64,16,128]{2,1,0:T(8,128)(2,1)S(1)} all-to-all(bf16[64,16,128]{2,1,0:T(8,128)(2,1)S(1)} %bitcast.30), channel_id=1, replica_groups=mesh['x'=4,'core'=2,'seq'=64] {'seq'}, dimensions={0} | all-to-all | bytes 524288 | tf_op jit(solution)/shard_map/all_to_all | solution.py:245
  33.1 0.0 copy-start.5
  33.1 12.8 %all_gather.3.same = bf16[4,512,128]{2,1,0:T(8,128)(2,1)S(1)} all-gather(bf16[1,512,128]{2,1,0:T(8,128)(2,1)S(1)} %get-tuple-element.3), channel_id=1, replica_groups=mesh['x'=4,'core'=2,'seq'=64] {'x'}, dimensions={0}, use_global_device_ids=true | all-gather | bytes 655360 | tf_op jit(solution)/shard_map/all_gather | solution.py:248
  45.9 0.0 copy-start.3
  45.9 0.0 copy-start.4
  45.9 2.0 %collective-permute-start = (bf16[4,512,128]{2,1,0:T(8,128)(2,1)S(1)}, bf16[4,512,128]{2,1,0:T(8,128)(2,1)S(1)}, u32[]{:S(2)}, u32[]{:S(2)}) collective-permute-start(bf16[4,512,128]{2,1,0:T(8,128)(2,1)S(1)} %all_gather.3.same), channel_id=1, source_target_pairs={{0,64},{64,0},{1,65},{65,1},{2,66},{66,2},{3,67},{67,3},{4,68},{68... | collective-permute-start | bytes 1572872 | tf_op jit(solution)/shard_map/ppermute | solution.py:249
  47.9 1.9 %collective-permute-done.other = bf16[4,512,128]{2,1,0:T(8,128)(2,1)S(1)} collective-permute-done((bf16[4,512,128]{2,1,0:T(8,128)(2,1)S(1)}, bf16[4,512,128]{2,1,0:T(8,128)(2,1)S(1)}, u32[]{:S(2)}, u32[]{:S(2)}) %collective-permute-start) | collective-permute-done | bytes 524320 | tf_op jit(solution)/shard_map/ppermute | solution.py:249
  49.8 0.0 copy-done.2
  49.8 0.0 copy-done
  49.8 0.0 copy-done.1
  49.8 0.0 copy-done.5
  49.8 0.0 copy-done.3
  49.8 0.0 copy-done.4
  49.8 4.7 %shard_map.95 = bf16[512,128]{1,0:T(8,128)(2,1)S(1)} custom-call(s32[9]{0:T(128)S(1)} %copy-done.4, s32[2,8]{1,0:T(2,128)S(1)} %copy-done.3, s32[2,8,8]{2,1,0:T(8,128)S(1)} %copy-done.2, f32[64]{0:T(128)S(1)} %copy-done.5, f32[64,4096]{1,0:T(8,128)S(1)} %copy-done, f32[64,4096]{1,0:T(8,128)S(1)} %copy-done.1, bf16[4,512,128]{2,1,0:T(8,128)(2,1)S(1)} %all_gather.3.same, ...), custom_call_target="tpu_custom_call" | custom-call | tf_op jit(solution)/shard_map/pallas_call | solution.py:212
  54.6 28.3 %all_to_all.11 = bf16[64,8,128]{2,1,0:T(8,128)(2,1)S(1)} all-to-all(bf16[64,8,128]{2,1,0:T(8,128)(2,1)S(1)} %bitcast.29), channel_id=1, replica_groups=mesh['x'=4,'core'=2,'seq'=64] {'seq'}, dimensions={0} | all-to-all | bytes 262144 | tf_op jit(solution)/shard_map/all_to_all | solution.py:251
  82.8 0.7 slice_bitcast_fusion.2
  (2 shorter events, 0.1 us)
Async XLA Ops:
  0.6 49.2 %copy-start.2 = (s32[2,8,8]{2,1,0:T(8,128)S(1)}, s32[2,8,8]{2,1,0:T(8,128)}, u32[]{:S(2)}) copy-start(s32[2,8,8]{2,1,0:T(8,128)} %mask.1) | copy-start | bytes 1540
  1.5 48.3 %copy-start = (f32[64,4096]{1,0:T(8,128)S(1)}, f32[64,4096]{1,0:T(8,128)}, u32[]{:S(2)}) copy-start(f32[64,4096]{1,0:T(8,128)} %q_gain.1) | copy-start | bytes 3145732
  1.6 48.3 %copy-start.1 = (f32[64,4096]{1,0:T(8,128)S(1)}, f32[64,4096]{1,0:T(8,128)}, u32[]{:S(2)}) copy-start(f32[64,4096]{1,0:T(8,128)} %k_gain.1) | copy-start | bytes 3145732
  33.1 16.7 %copy-start.5 = (f32[64]{0:T(128)S(1)}, f32[64]{0:T(128)}, u32[]{:S(2)}) copy-start(f32[64]{0:T(128)} %delta.1) | copy-start | bytes 772
  45.9 4.0 %copy-start.3 = (s32[2,8]{1,0:T(2,128)S(1)}, s32[2,8]{1,0:T(2,128)}, u32[]{:S(2)}) copy-start(s32[2,8]{1,0:T(2,128)} %steps.1) | copy-start | bytes 196
  45.9 4.0 %copy-start.4 = (s32[9]{0:T(128)S(1)}, s32[9]{0:T(128)}, u32[]{:S(2)}) copy-start(s32[9]{0:T(128)} %counts.1) | copy-start | bytes 112
  45.9 3.9 %collective-permute-start = (bf16[4,512,128]{2,1,0:T(8,128)(2,1)S(1)}, bf16[4,512,128]{2,1,0:T(8,128)(2,1)S(1)}, u32[]{:S(2)}, u32[]{:S(2)}) collective-permute-start(bf16[4,512,128]{2,1,0:T(8,128)(2,1)S(1)} %all_gather.3.same), channel_id=1, source_target_pairs={{0,64},{64,0},{1,65},{65,1},{2,66},{66,2},{3,67},{67,3},{4,68},{68... | collective-permute-start | bytes 1572872 | tf_op jit(solution)/shard_map/ppermute | solution.py:249

commit v2 on v1

v2 whole, which is shorter than its diff:
```python
import functools
import math

import jax
import jax.numpy as jnp
from jax import lax
from jax.experimental import pallas as pl
from jax.experimental.pallas import tpu as pltpu
from jax.sharding import Mesh
from jax.sharding import PartitionSpec as P

HEAD_DIM = 128
SPAN = 512
SPANS = 8
KEYS = 128
PER_SPAN = SPAN // KEYS
NONE = SPANS * PER_SPAN
GROUP = 4
ENTERING, MIDDLE, UNUSED = SPANS, SPANS + 1, SPANS + 2
SCORE_SCALE = math.log2(math.e) / math.sqrt(HEAD_DIM)
SHIFT = 40.0
SMALL = 2.0**-60


def normed(x):
    x = x.astype(jnp.float32)
    return x * lax.rsqrt(jnp.mean(x * x, axis=-1, keepdims=True) + 1e-06)


def head_kernel(
    place,
    counts,
    steps,
    mask,
    delta,
    q_gain,
    k_gain,
    same,
    other,
    fresh,
    out,
    qg,
    kg,
    xs,
    query,
    key,
    value,
    query2,
    key2,
    value2,
    acc,
    top,
    least,
    blocks,
    todo,
    shares,
    sems,
):
    g, half, head, core = place()
    cols = pl.ds(pl.multiple_of(head * HEAD_DIM, HEAD_DIM), HEAD_DIM)
    copies = [
        pltpu.make_async_copy(q_gain.at[:, cols], qg, sems.at[0]),
        pltpu.make_async_copy(k_gain.at[:, cols], kg, sems.at[1]),
    ]
    for copy in copies:
        copy.start()
    for keys, values in ((key, value), (key2, value2)):
        keys[NONE] = jnp.zeros((HEAD_DIM, KEYS), jnp.bfloat16)
        values[NONE] = jnp.zeros((KEYS, 2 * HEAD_DIM), jnp.bfloat16)

    def put_values(x, live, i, values):
        alive = lax.broadcasted_iota(jnp.int32, (SPAN, HEAD_DIM), 0) < live
        kept = jnp.where(alive, x.astype(jnp.float32), 0.0).astype(jnp.bfloat16)
        ones = jnp.where(alive, 1.0, 0.0).astype(jnp.bfloat16)
        for r in range(PER_SPAN):
            values[PER_SPAN * i + r, :, :HEAD_DIM] = kept[r * KEYS : (r + 1) * KEYS]
            values[PER_SPAN * i + r, :, HEAD_DIM:] = ones[r * KEYS : (r + 1) * KEYS]

    def put_keys(n, t, i, keys):
        turned = (n * kg[pl.ds(t, 1), :]).astype(jnp.bfloat16).T
        for r in range(PER_SPAN):
            keys[PER_SPAN * i + r] = turned[:, r * KEYS : (r + 1) * KEYS]

    def make_query(n, t):
        return (n * qg[pl.ds(t, 1), :]).astype(jnp.bfloat16)

    last = jnp.minimum(g + 1, SPANS - 1)

    def each_pair(step):
        for a in range(SPANS // 2):

            @pl.when(2 * a <= last)
            def _():
                for source, j in ((same, 2 * a + core), (other, 2 * a + 1 - core)):
                    step(source[a], j)

    def values_of(x, j):
        xs[j] = x
        put_values(x, counts[j], j, value)

    def keys_of(x, j):
        t = steps[0, j]
        n = normed(x)
        put_keys(n, t, j, key)
        query[j] = make_query(n, t)

    each_pair(values_of)
    for copy in copies:
        copy.wait()
    each_pair(keys_of)

    def list_blocks(seen, live):
        size = jnp.int32(0)
        for i in range(SPANS):
            for r in range(PER_SPAN):
                blocks[size + r] = PER_SPAN * i + r
            size += jnp.where(seen(i) > 0, (live(i) + KEYS - 1) // KEYS, 0)
        for r in range(2 * GROUP):
            blocks[size + r] = NONE
        return size

    def group(q, keys, values, first, pairs):
        weights, parts = [], []
        for r in range(pairs):
            left, right = blocks[first + 2 * r], blocks[first + 2 * r + 1]
            score = jnp.dot(
                q, jnp.concatenate([keys[left], keys[right]], axis=1), preferred_element_type=jnp.float32
            )
            weights.append(jnp.exp2(score * SCORE_SCALE - SHIFT).astype(jnp.bfloat16))
        for r in range(pairs):
            left, right = blocks[first + 2 * r], blocks[first + 2 * r + 1]
            parts.append(
                jnp.dot(
                    weights[r],
                    jnp.concatenate([values[left], values[right]], axis=0),
                    preferred_element_type=jnp.float32,
                )
            )
        return sum(parts[1:], parts[0])

    def attend(q, rows, keys, values, size, slot):
        acc[slot, :rows] = group(q, keys, values, 0, GROUP)
        if rows < SPAN:
            acc[slot, rows:] = jnp.ones((SPAN - rows, 2 * HEAD_DIM), jnp.float32)
        rest = jnp.maximum((size + 1) // 2 - GROUP, 0)
        whole = (rest + 1) // GROUP

        def more(n, carry):
            acc[slot, :rows] += group(q, keys, values, 2 * GROUP * (n + 1), GROUP)
            return carry

        lax.fori_loop(0, whole, more, 0)

        @pl.when(rest > GROUP * whole)
        def _():
            acc[slot, :rows] += group(q, keys, values, 2 * GROUP * (whole + 1), GROUP // 2)

    def attend_safe(q, keys, values, size, live, slot):
        def scores(b):
            score = jnp.dot(q, keys[b], preferred_element_type=jnp.float32) * SCORE_SCALE
            at = lax.broadcasted_iota(jnp.int32, (SPAN, KEYS), 1) + lax.rem(b, PER_SPAN) * KEYS
            return jnp.where(at < live(b // PER_SPAN), score, -1e30)

        def highest(n, carry):
            top[...] = jnp.maximum(top[...], jnp.max(scores(blocks[n]), axis=-1, keepdims=True))
            return carry

        def add(n, carry):
            weight = jnp.exp2(scores(blocks[n]) - top[...]).astype(jnp.bfloat16)
            acc[slot] += jnp.dot(weight, values[blocks[n]], preferred_element_type=jnp.float32)
            return carry

        top[...] = jnp.full((SPAN, KEYS), -1e30, jnp.float32)
        acc[slot] = jnp.zeros((SPAN, 2 * HEAD_DIM), jnp.float32)
        lax.fori_loop(0, size, highest, 0)
        lax.fori_loop(0, size, add, 0)

    def attended(slot):
        total = acc[slot, :, HEAD_DIM:]
        return acc[slot, :, :HEAD_DIM] / jnp.where(total > 0.0, total, 1.0), total

    def moved(x, target, rate):
        old = x.astype(jnp.float32)
        return old + rate * (target - old)

    def enter(j, slot, counted=True):
        target, total = attended(slot)
        smallest = jnp.min(total.reshape(SPAN // 8, 8, HEAD_DIM), axis=0)
        least[...] = jnp.minimum(least[...], jnp.where(counted, smallest, 1.0))
        target = target.astype(jnp.bfloat16).astype(jnp.float32)
        x = moved(xs[j], target, delta[steps[0, j]]).astype(jnp.bfloat16)
        e = jnp.maximum(j - 1, 0)
        t = steps[1, e]
        n = normed(x)
        put_values(x, counts[j], e, value2)
        put_keys(n, t, e, key2)
        xs[jnp.where(j == g + 1, ENTERING, jnp.where(j == g, MIDDLE, UNUSED))] = x
        query2[jnp.where(j == g + 1, 0, 1)] = make_query(n, t)

    def blocks_of(j):
        return list_blocks(lambda i: mask[0, j, i], lambda i: counts[i])

    lives = [(counts[i] + KEYS - 1) // KEYS for i in range(SPANS + 1)]
    todo[0] = g + 1
    wanted = jnp.where(g < SPANS - 1, 1, 0)
    loads = [jnp.int32(0), PER_SPAN * counts[jnp.minimum(g + 1, SPANS)] // KEYS]
    shares[SPANS - 1] = jnp.where(jnp.logical_and(half == 1, g == SPANS - 1), 1, 0)
    for j in reversed(range(SPANS)):
        own = j == g
        read = jnp.logical_and(j <= g, mask[1, g, j - 1] > 0) if j > 0 else jnp.bool_(False)
        cost = sum(jnp.where(mask[0, j, i] > 0, lives[i], 0) for i in range(j + 1))
        cost = jnp.where(own, PER_SPAN, lives[j]) * cost + PER_SPAN * lives[j] + PER_SPAN
        maker = jnp.where(jnp.logical_or(own, loads[0] <= loads[1]), 0, 1)
        made = jnp.logical_or(own, read)
        for k in range(2):
            loads[k] += jnp.where(jnp.logical_and(made, maker == k), cost, 0)
        mine = jnp.logical_and(made, maker == half)
        todo[wanted] = j
        wanted += jnp.where(mine, 1, 0)
        if j > 0:
            last_one = jnp.logical_and(half == 1, j - 1 == g)
            shares[j - 1] = jnp.where(jnp.logical_or(jnp.logical_and(mine, read), last_one), 1, 0)

    least[...] = jnp.ones((8, HEAD_DIM), jnp.float32)

    def one(m, carry):
        j, before = todo[m], todo[jnp.maximum(m - 1, 0)]
        size = blocks_of(j)
        slot = lax.rem(m, 2)

        def block(rows):
            enter(before, 1 - slot, m > 0)
            attend(query[j, :rows], rows, key, value, size, slot)

        rows = jnp.where(jnp.logical_or(j == g + 1, j == g), SPAN, counts[j])
        for r in range(2, PER_SPAN + 1):
            fits = rows <= r * KEYS
            if r > 2:
                fits = jnp.logical_and(fits, rows > (r - 1) * KEYS)
            pl.when(fits)(functools.partial(block, r * KEYS))
        return carry

    lax.fori_loop(0, wanted, one, 0)

    @pl.when(wanted > 0)
    def _():
        enter(todo[wanted - 1], lax.rem(wanted - 1, 2))

    @pl.when(jnp.min(least[...]) < SMALL)
    def _():
        def one_safe(m, carry):
            j = todo[m]
            attend_safe(query[j], key, value, blocks_of(j), lambda i: counts[i], 0)
            enter(j, 0)
            return carry

        lax.fori_loop(0, wanted, one_safe, 0)

    @pl.when(g == SPANS - 1)
    def _():
        x = fresh[...]
        xs[ENTERING] = x
        t = steps[1, g]
        n = normed(x)
        put_values(x, counts[SPANS], SPANS - 1, value2)
        put_keys(n, t, SPANS - 1, key2)
        query2[0] = make_query(n, t)

    size = list_blocks(lambda e: shares[e], lambda e: counts[e + 1])
    rate = delta[steps[1, g]]

    def put(row, x):
        out[:, row : row + 8] = x.reshape(SPAN // 8, 8, HEAD_DIM).astype(jnp.bfloat16)

    def put_final(scale):
        target, total = attended(0)
        put(8, moved(xs[ENTERING], target, rate))
        put(16, jnp.where(total > 0.0, jnp.sqrt(total) * scale, 0.0))
        return jnp.min(total)

    put(0, xs[MIDDLE].astype(jnp.float32))
    attend(query2[0], SPAN, key2, value2, size, 0)

    @pl.when(jnp.logical_and(put_final(2.0 ** (SHIFT / 2)) < SMALL, size > 0))
    def _():
        attend_safe(query2[0], key2, value2, size, lambda e: counts[e + 1], 0)
        put_final(jnp.exp2(top[...] * 0.5))


def mesh_place():
    seq = lax.axis_index("seq")
    core = lax.axis_index("core")
    return 2 * lax.axis_index("x") + core, lax.rem(seq, 2), seq // 2, core


def both_steps(place, counts, steps, mask, delta, q_gain, k_gain, same, other, fresh, interpret=False):
    smem = pl.BlockSpec(memory_space=pltpu.SMEM)
    hbm = pl.BlockSpec(memory_space=pl.ANY)
    vmem = pl.BlockSpec(memory_space=pltpu.VMEM)
    noise_steps = q_gain.shape[0]
    bf16, f32 = jnp.bfloat16, jnp.float32
    return pl.pallas_call(
        functools.partial(head_kernel, place),
        out_shape=jax.ShapeDtypeStruct((SPAN // 8, 24, HEAD_DIM), bf16),
        in_specs=[smem, smem, smem, smem, hbm, hbm, vmem, vmem, vmem],
        out_specs=vmem,
        scratch_shapes=[
            pltpu.VMEM((noise_steps, HEAD_DIM), f32),
            pltpu.VMEM((noise_steps, HEAD_DIM), f32),
            pltpu.VMEM((UNUSED + 1, SPAN, HEAD_DIM), bf16),
            pltpu.VMEM((SPANS, SPAN, HEAD_DIM), bf16),
            pltpu.VMEM((NONE + 1, HEAD_DIM, KEYS), bf16),
            pltpu.VMEM((NONE + 1, KEYS, 2 * HEAD_DIM), bf16),
            pltpu.VMEM((2, SPAN, HEAD_DIM), bf16),
            pltpu.VMEM((NONE + 1, HEAD_DIM, KEYS), bf16),
            pltpu.VMEM((NONE + 1, KEYS, 2 * HEAD_DIM), bf16),
            pltpu.VMEM((2, SPAN, 2 * HEAD_DIM), f32),
            pltpu.VMEM((SPAN, KEYS), f32),
            pltpu.VMEM((8, HEAD_DIM), f32),
            pltpu.SMEM((NONE + 2 * GROUP,), jnp.int32),
            pltpu.SMEM((SPANS + 2,), jnp.int32),
            pltpu.SMEM((SPANS,), jnp.int32),
            pltpu.SemaphoreType.DMA((2,)),
        ],
        compiler_params=pltpu.CompilerParams(vmem_limit_bytes=32 * 1024 * 1024),
        interpret=interpret,
    )(counts, steps, mask, delta, q_gain, k_gain, same, other, fresh)


def per_device(latents, new_span, counts, steps, span_mask, q_gain, k_gain, delta):
    rows, width = latents.shape
    heads = width // HEAD_DIM

    def to_heads(block):
        return block.reshape(rows, heads, HEAD_DIM).transpose(1, 0, 2)

    sent = jnp.concatenate([to_heads(latents), to_heads(new_span)], axis=1)
    sent = jnp.broadcast_to(sent[:, None], (heads, 2, 2 * rows, HEAD_DIM)).reshape(2 * heads, 2 * rows, HEAD_DIM)
    got = lax.all_to_all(sent, "seq", 0, 0, tiled=True)
    mine = got[:, :rows].reshape(SPAN, HEAD_DIM)
    fresh = got[:, rows:].reshape(SPAN, HEAD_DIM)
    same = lax.all_gather(mine, "x", axis=0)
    other = lax.ppermute(same, "core", [(0, 1), (1, 0)])
    done = both_steps(mesh_place, counts, steps, span_mask, delta, q_gain, k_gain, same, other, fresh)
    back = lax.all_to_all(done, "seq", 0, 0, tiled=True)
    back = back.reshape(heads, 2, 3 * rows, HEAD_DIM)

    def to_tokens(block):
        return block.transpose(1, 0, 2).reshape(rows, width)

    part = back[:, :, rows : 2 * rows].astype(jnp.float32)
    root = back[:, :, 2 * rows :].astype(jnp.float32)
    ratio = root[:, 0] / root[:, 1]
    share = 1.0 / (1.0 + ratio * ratio)
    final = part[:, 0] + share * (part[:, 1] - part[:, 0])
    return to_tokens(back[:, 0, :rows]), to_tokens(final.astype(jnp.bfloat16))


def solution(mesh):
    mesh = Mesh(mesh.devices.reshape(4, 2, 64), ("x", "core", "seq"))
    tokens = P(("x", "core", "seq"), None)
    in_specs = (tokens, P("seq", None), P(), P(), P(), P(), P(), P())
    return jax.shard_map(per_device, mesh=mesh, in_specs=in_specs, out_specs=(tokens, tokens), check_vma=False)
```

time: 84.6 us -> 82.6 us (0.976)
  blocking collectives: 72.5 us -> 64.9 us
  Pallas kernels: 4.73 us -> 10.4 us
    all_to_all x1, blocking collectives: 28.3 us -> 20.7 us  [per_device(): back = lax.all_to_all(done, 'seq', 0, 0, tiled=True)]
    pallas_call x1, Pallas kernels: 4.73 us -> 10.4 us  [both_steps(): pl.pallas_call(functools.partial(head_kernel, place), out_shape=jax.Shape...]
where the time goes in v2:
time: 82.6 us; the launch traced here: 82.3 us
  blocking collectives  64.9 us (79%)
  Pallas kernels  10.4 us (13%)
  starting transfers between devices  2.04 us (2%)
  waiting for transfers between devices  1.88 us (2%)
  other arithmetic  1.64 us (2%)
    all_to_all x1, blocking collectives, per_device(): got = lax.all_to_all(sent, 'seq', 0, 0, tiled=True)  31.4 us
    all_to_all x1, blocking collectives, per_device(): back = lax.all_to_all(done, 'seq', 0, 0, tiled=True)  20.7 us
    all_gather x1, blocking collectives, per_device(): same = lax.all_gather(mine, 'x', axis=0)  12.8 us
    pallas_call x1, Pallas kernels, both_steps(): pl.pallas_call(functools.partial(head_kernel, place), out_shape=jax.Shape...  10.4 us
    ppermute x1, starting transfers between devices, per_device(): other = lax.ppermute(same, 'core', [(0, 1), (1, 0)])  2.04 us
    ppermute x1, waiting for transfers between devices, per_device(): other = lax.ppermute(same, 'core', [(0, 1), (1, 0)])  1.88 us
  transfers between devices with their start and end apart: 1, of which 1 were waited for; matrix products, arithmetic and copies ran while one was open for 0% of the time, Pallas kernels for 0%

profile of v2, /device:TPU:6, one launch (start us, length us, event | category | flops | bytes accessed | tf_op | source)
XLA Modules:
  0.0 82.3 jit_solution(10457736806704695250)
XLA Ops:
  0.6 0.0 copy-start.2
  0.6 0.9 %pad_maximum_fusion = bf16[32,16,128]{2,1,0:T(8,128)(2,1)S(1)} fusion(bf16[32,8,128]{2,1,0:T(8,128)(2,1)} %bitcast.47, bf16[32,8,128]{2,1,0:T(8,128)(2,1)} %bitcast.48), kind=kLoop, calls=%fused_computation.13 | loop fusion | flops 262144 | bytes 262144 | tf_op jit(solution)/shard_map/concatenate | solution.py:337
  1.5 0.0 copy-start
  1.6 0.0 copy-start.1
  1.6 31.4 %all_to_all.10 = bf16[64,16,128]{2,1,0:T(8,128)(2,1)S(1)} all-to-all(bf16[64,16,128]{2,1,0:T(8,128)(2,1)S(1)} %bitcast.46), channel_id=1, replica_groups=mesh['x'=4,'core'=2,'seq'=64] {'seq'}, dimensions={0} | all-to-all | bytes 524288 | tf_op jit(solution)/shard_map/all_to_all | solution.py:339
  33.1 0.0 copy-start.5
  33.1 12.8 %all_gather.3.same = bf16[4,512,128]{2,1,0:T(8,128)(2,1)S(1)} all-gather(bf16[1,512,128]{2,1,0:T(8,128)(2,1)S(1)} %get-tuple-element.5), channel_id=1, replica_groups=mesh['x'=4,'core'=2,'seq'=64] {'x'}, dimensions={0}, use_global_device_ids=true | all-gather | bytes 655360 | tf_op jit(solution)/shard_map/all_gather | solution.py:342
  45.9 0.0 copy-start.3
  45.9 0.0 copy-start.4
  45.9 2.0 %collective-permute-start = (bf16[4,512,128]{2,1,0:T(8,128)(2,1)S(1)}, bf16[4,512,128]{2,1,0:T(8,128)(2,1)S(1)}, u32[]{:S(2)}, u32[]{:S(2)}) collective-permute-start(bf16[4,512,128]{2,1,0:T(8,128)(2,1)S(1)} %all_gather.3.same), channel_id=1, source_target_pairs={{0,64},{64,0},{1,65},{65,1},{2,66},{66,2},{3,67},{67,3},{4,68},{68... | collective-permute-start | bytes 1572872 | tf_op jit(solution)/shard_map/ppermute | solution.py:343
  47.9 1.9 %collective-permute-done.other = bf16[4,512,128]{2,1,0:T(8,128)(2,1)S(1)} collective-permute-done((bf16[4,512,128]{2,1,0:T(8,128)(2,1)S(1)}, bf16[4,512,128]{2,1,0:T(8,128)(2,1)S(1)}, u32[]{:S(2)}, u32[]{:S(2)}) %collective-permute-start) | collective-permute-done | bytes 524320 | tf_op jit(solution)/shard_map/ppermute | solution.py:343
  49.8 0.0 copy-done.2
  49.8 0.0 copy-done
  49.8 0.0 copy-done.1
  49.8 0.0 copy-done.5
  49.8 0.0 copy-done.3
  49.8 0.0 copy-done.4
  49.8 10.4 %shard_map.95 = bf16[64,24,128]{2,1,0:T(8,128)(2,1)S(1)} custom-call(s32[9]{0:T(128)S(1)} %copy-done.4, s32[2,8]{1,0:T(2,128)S(1)} %copy-done.3, s32[2,8,8]{2,1,0:T(8,128)S(1)} %copy-done.2, f32[64]{0:T(128)S(1)} %copy-done.5, f32[64,4096]{1,0:T(8,128)S(1)} %copy-done, f32[64,4096]{1,0:T(8,128)S(1)} %copy-done.1, bf16[4,512,128]{2,1,0:T(8,128)(2,1)S(1)} %all_gather.3.same, ...), custom_call_target="tpu_custom_call" | custom-call | tf_op jit(solution)/shard_map/pallas_call | solution.py:302
  60.3 20.7 %all_to_all.11 = bf16[64,24,128]{2,1,0:T(8,128)(2,1)S(1)} all-to-all(bf16[64,24,128]{2,1,0:T(8,128)(2,1)S(1)} %shard_map.95), channel_id=1, replica_groups=mesh['x'=4,'core'=2,'seq'=64] {'seq'}, dimensions={0} | all-to-all | bytes 786432 | tf_op jit(solution)/shard_map/all_to_all | solution.py:345
  80.9 0.6 slice_bitcast_fusion.4
  81.6 0.7 fusion.7
  (4 shorter events, 0.1 us)
Async XLA Ops:
  0.6 49.2 %copy-start.2 = (s32[2,8,8]{2,1,0:T(8,128)S(1)}, s32[2,8,8]{2,1,0:T(8,128)}, u32[]{:S(2)}) copy-start(s32[2,8,8]{2,1,0:T(8,128)} %mask.1) | copy-start | bytes 1540
  1.5 48.3 %copy-start = (f32[64,4096]{1,0:T(8,128)S(1)}, f32[64,4096]{1,0:T(8,128)}, u32[]{:S(2)}) copy-start(f32[64,4096]{1,0:T(8,128)} %q_gain.1) | copy-start | bytes 3145732
  1.6 48.3 %copy-start.1 = (f32[64,4096]{1,0:T(8,128)S(1)}, f32[64,4096]{1,0:T(8,128)}, u32[]{:S(2)}) copy-start(f32[64,4096]{1,0:T(8,128)} %k_gain.1) | copy-start | bytes 3145732
  33.1 16.7 %copy-start.5 = (f32[64]{0:T(128)S(1)}, f32[64]{0:T(128)}, u32[]{:S(2)}) copy-start(f32[64]{0:T(128)} %delta.1) | copy-start | bytes 772
  45.9 4.0 %copy-start.3 = (s32[2,8]{1,0:T(2,128)S(1)}, s32[2,8]{1,0:T(2,128)}, u32[]{:S(2)}) copy-start(s32[2,8]{1,0:T(2,128)} %steps.1) | copy-start | bytes 196
  45.9 4.0 %copy-start.4 = (s32[9]{0:T(128)S(1)}, s32[9]{0:T(128)}, u32[]{:S(2)}) copy-start(s32[9]{0:T(128)} %counts.1) | copy-start | bytes 112
  45.9 3.9 %collective-permute-start = (bf16[4,512,128]{2,1,0:T(8,128)(2,1)S(1)}, bf16[4,512,128]{2,1,0:T(8,128)(2,1)S(1)}, u32[]{:S(2)}, u32[]{:S(2)}) collective-permute-start(bf16[4,512,128]{2,1,0:T(8,128)(2,1)S(1)} %all_gather.3.same), channel_id=1, source_target_pairs={{0,64},{64,0},{1,65},{65,1},{2,66},{66,2},{3,67},{67,3},{4,68},{68... | collective-permute-start | bytes 1572872 | tf_op jit(solution)/shard_map/ppermute | solution.py:343

commit v3 on v2

--- a/solution.py
+++ b/solution.py
@@ -12,11 +12,12 @@
 HEAD_DIM = 128
 SPAN = 512
 SPANS = 8
+HALF = SPAN // 2
 KEYS = 128
 PER_SPAN = SPAN // KEYS
 NONE = SPANS * PER_SPAN
 GROUP = 4
-ENTERING, MIDDLE, UNUSED = SPANS, SPANS + 1, SPANS + 2
+ENTERING, MIDDLE, UNUSED = 0, 1, 2
 SCORE_SCALE = math.log2(math.e) / math.sqrt(HEAD_DIM)
 SHIFT = 40.0
 SMALL = 2.0**-60
@@ -53,7 +54,7 @@
     least,
     blocks,
     todo,
-    shares,
+    sent,
     sems,
 ):
     g, half, head, core = place()
@@ -155,71 +156,58 @@
         def _():
             acc[slot, :rows] += group(q, keys, values, 2 * GROUP * (whole + 1), GROUP // 2)
 
-    def attend_safe(q, keys, values, size, live, slot):
+    def attend_safe(q, rows, keys, values, size, live, slot):
         def scores(b):
             score = jnp.dot(q, keys[b], preferred_element_type=jnp.float32) * SCORE_SCALE
-            at = lax.broadcasted_iota(jnp.int32, (SPAN, KEYS), 1) + lax.rem(b, PER_SPAN) * KEYS
+            at = lax.broadcasted_iota(jnp.int32, (rows, KEYS), 1) + lax.rem(b, PER_SPAN) * KEYS
             return jnp.where(at < live(b // PER_SPAN), score, -1e30)
 
         def highest(n, carry):
-            top[...] = jnp.maximum(top[...], jnp.max(scores(blocks[n]), axis=-1, keepdims=True))
+            top[:rows] = jnp.maximum(top[:rows], jnp.max(scores(blocks[n]), axis=-1, keepdims=True))
             return carry
 
         def add(n, carry):
-            weight = jnp.exp2(scores(blocks[n]) - top[...]).astype(jnp.bfloat16)
-            acc[slot] += jnp.dot(weight, values[blocks[n]], preferred_element_type=jnp.float32)
+            weight = jnp.exp2(scores(blocks[n]) - top[:rows]).astype(jnp.bfloat16)
+            acc[slot, :rows] += jnp.dot(weight, values[blocks[n]], preferred_element_type=jnp.float32)
             return carry
 
-        top[...] = jnp.full((SPAN, KEYS), -1e30, jnp.float32)
-        acc[slot] = jnp.zeros((SPAN, 2 * HEAD_DIM), jnp.float32)
+        top[:rows] = jnp.full((rows, KEYS), -1e30, jnp.float32)
+        acc[slot, :rows] = jnp.zeros((rows, 2 * HEAD_DIM), jnp.float32)
         lax.fori_loop(0, size, highest, 0)
         lax.fori_loop(0, size, add, 0)
 
-    def attended(slot):
-        total = acc[slot, :, HEAD_DIM:]
-        return acc[slot, :, :HEAD_DIM] / jnp.where(total > 0.0, total, 1.0), total
-
-    def moved(x, target, rate):
+    def finish(x, rows, slot, rate):
+        total = acc[slot, :rows, HEAD_DIM:]
+        target = (acc[slot, :rows, :HEAD_DIM] / total).astype(jnp.bfloat16).astype(jnp.float32)
         old = x.astype(jnp.float32)
-        return old + rate * (target - old)
+        return (old + rate * (target - old)).astype(jnp.bfloat16), total
+
+    def sent_rows(x):
+        pieces = x.astype(jnp.float32).reshape(SPAN // 16, 2, 8, HEAD_DIM)
+        return jnp.where(half == 0, pieces[:, 0], pieces[:, 1])
 
     def enter(j, slot, counted=True):
-        target, total = attended(slot)
+        x, total = finish(xs[j], SPAN, slot, delta[steps[0, j]])
         smallest = jnp.min(total.reshape(SPAN // 8, 8, HEAD_DIM), axis=0)
         least[...] = jnp.minimum(least[...], jnp.where(counted, smallest, 1.0))
-        target = target.astype(jnp.bfloat16).astype(jnp.float32)
-        x = moved(xs[j], target, delta[steps[0, j]]).astype(jnp.bfloat16)
-        e = jnp.maximum(j - 1, 0)
+        e = jnp.where(j > 0, j - 1, SPANS - 1)
         t = steps[1, e]
         n = normed(x)
         put_values(x, counts[j], e, value2)
         put_keys(n, t, e, key2)
-        xs[jnp.where(j == g + 1, ENTERING, jnp.where(j == g, MIDDLE, UNUSED))] = x
-        query2[jnp.where(j == g + 1, 0, 1)] = make_query(n, t)
+        sent[jnp.where(j == g + 1, ENTERING, jnp.where(j == g, MIDDLE, UNUSED))] = sent_rows(x)
+        query2[jnp.where(j == g + 1, 0, 1)] = make_query(sent_rows(n).reshape(HALF, HEAD_DIM), t)
 
     def blocks_of(j):
         return list_blocks(lambda i: mask[0, j, i], lambda i: counts[i])
 
-    lives = [(counts[i] + KEYS - 1) // KEYS for i in range(SPANS + 1)]
     todo[0] = g + 1
     wanted = jnp.where(g < SPANS - 1, 1, 0)
-    loads = [jnp.int32(0), PER_SPAN * counts[jnp.minimum(g + 1, SPANS)] // KEYS]
-    shares[SPANS - 1] = jnp.where(jnp.logical_and(half == 1, g == SPANS - 1), 1, 0)
-    for j in reversed(range(SPANS)):
-        own = j == g
-        read = jnp.logical_and(j <= g, mask[1, g, j - 1] > 0) if j > 0 else jnp.bool_(False)
-        cost = sum(jnp.where(mask[0, j, i] > 0, lives[i], 0) for i in range(j + 1))
-        cost = jnp.where(own, PER_SPAN, lives[j]) * cost + PER_SPAN * lives[j] + PER_SPAN
-        maker = jnp.where(jnp.logical_or(own, loads[0] <= loads[1]), 0, 1)
-        made = jnp.logical_or(own, read)
-        for k in range(2):
-            loads[k] += jnp.where(jnp.logical_and(made, maker == k), cost, 0)
-        mine = jnp.logical_and(made, maker == half)
+    todo[wanted] = g
+    wanted += 1
+    for j in range(1, SPANS):
         todo[wanted] = j
-        wanted += jnp.where(mine, 1, 0)
-        if j > 0:
-            last_one = jnp.logical_and(half == 1, j - 1 == g)
-            shares[j - 1] = jnp.where(jnp.logical_or(jnp.logical_and(mine, read), last_one), 1, 0)
+        wanted += jnp.where(jnp.logical_and(j < g, mask[1, g, j - 1] > 0), 1, 0)
 
     least[...] = jnp.ones((8, HEAD_DIM), jnp.float32)
 
@@ -241,16 +229,13 @@
         return carry
 
     lax.fori_loop(0, wanted, one, 0)
-
-    @pl.when(wanted > 0)
-    def _():
-        enter(todo[wanted - 1], lax.rem(wanted - 1, 2))
+    enter(todo[wanted - 1], lax.rem(wanted - 1, 2))
 
     @pl.when(jnp.min(least[...]) < SMALL)
     def _():
         def one_safe(m, carry):
             j = todo[m]
-            attend_safe(query[j], key, value, blocks_of(j), lambda i: counts[i], 0)
+            attend_safe(query[j], SPAN, key, value, blocks_of(j), lambda i: counts[i], 0)
             enter(j, 0)
             return carry
 
@@ -259,38 +244,31 @@
     @pl.when(g == SPANS - 1)
     def _():
         x = fresh[...]
-        xs[ENTERING] = x
         t = steps[1, g]
         n = normed(x)
         put_values(x, counts[SPANS], SPANS - 1, value2)
         put_keys(n, t, SPANS - 1, key2)
-        query2[0] = make_query(n, t)
-
-    size = list_blocks(lambda e: shares[e], lambda e: counts[e + 1])
-    rate = delta[steps[1, g]]
-
-    def put(row, x):
-        out[:, row : row + 8] = x.reshape(SPAN // 8, 8, HEAD_DIM).astype(jnp.bfloat16)
-
-    def put_final(scale):
-        target, total = attended(0)
-        put(8, moved(xs[ENTERING], target, rate))
-        put(16, jnp.where(total > 0.0, jnp.sqrt(total) * scale, 0.0))
+        sent[ENTERING] = sent_rows(x)
+        query2[0] = make_query(sent_rows(n).reshape(HALF, HEAD_DIM), t)
+
+    size = list_blocks(lambda e: mask[1, g, e], lambda e: counts[e + 1])
+    out[:, :8] = sent[MIDDLE].astype(jnp.bfloat16)
+    attend(query2[0], HALF, key2, value2, size, 0)
+
+    def put_final():
+        x, total = finish(sent[ENTERING].reshape(HALF, HEAD_DIM), HALF, 0, delta[steps[1, g]])
+        out[:, 8:] = x.astype(jnp.float32).reshape(SPAN // 16, 8, HEAD_DIM).astype(jnp.bfloat16)
         return jnp.min(total)
 
-    put(0, xs[MIDDLE].astype(jnp.float32))
-    attend(query2[0], SPAN, key2, value2, size, 0)
-
-    @pl.when(jnp.logical_and(put_final(2.0 ** (SHIFT / 2)) < SMALL, size > 0))
+    @pl.when(put_final() < SMALL)
     def _():
-        attend_safe(query2[0], key2, value2, size, lambda e: counts[e + 1], 0)
-        put_final(jnp.exp2(top[...] * 0.5))
+        attend_safe(query2[0], HALF, key2, value2, size, lambda e: counts[e + 1], 0)
+        put_final()
 
 
 def mesh_place():
-    seq = lax.axis_index("seq")
     core = lax.axis_index("core")
-    return 2 * lax.axis_index("x") + core, lax.rem(seq, 2), seq // 2, core
+    return 2 * lax.axis_index("x") + core, lax.axis_index("half"), lax.axis_index("head"), core
 
 
 def both_steps(place, counts, steps, mask, delta, q_gain, k_gain, same, other, fresh, interpret=False):
@@ -301,17 +279,17 @@
     bf16, f32 = jnp.bfloat16, jnp.float32
     return pl.pallas_call(
         functools.partial(head_kernel, place),
-        out_shape=jax.ShapeDtypeStruct((SPAN // 8, 24, HEAD_DIM), bf16),
+        out_shape=jax.ShapeDtypeStruct((SPAN // 16, 16, HEAD_DIM), bf16),
         in_specs=[smem, smem, smem, smem, hbm, hbm, vmem, vmem, vmem],
         out_specs=vmem,
         scratch_shapes=[
             pltpu.VMEM((noise_steps, HEAD_DIM), f32),
             pltpu.VMEM((noise_steps, HEAD_DIM), f32),
-            pltpu.VMEM((UNUSED + 1, SPAN, HEAD_DIM), bf16),
+            pltpu.VMEM((SPANS, SPAN, HEAD_DIM), bf16),
             pltpu.VMEM((SPANS, SPAN, HEAD_DIM), bf16),
             pltpu.VMEM((NONE + 1, HEAD_DIM, KEYS), bf16),
             pltpu.VMEM((NONE + 1, KEYS, 2 * HEAD_DIM), bf16),
-            pltpu.VMEM((2, SPAN, HEAD_DIM), bf16),
+            pltpu.VMEM((2, HALF, HEAD_DIM), bf16),
             pltpu.VMEM((NONE + 1, HEAD_DIM, KEYS), bf16),
             pltpu.VMEM((NONE + 1, KEYS, 2 * HEAD_DIM), bf16),
             pltpu.VMEM((2, SPAN, 2 * HEAD_DIM), f32),
@@ -319,7 +297,7 @@
             pltpu.VMEM((8, HEAD_DIM), f32),
             pltpu.SMEM((NONE + 2 * GROUP,), jnp.int32),
             pltpu.SMEM((SPANS + 2,), jnp.int32),
-            pltpu.SMEM((SPANS,), jnp.int32),
+            pltpu.VMEM((UNUSED + 1, SPAN // 16, 8, HEAD_DIM), f32),
             pltpu.SemaphoreType.DMA((2,)),
         ],
         compiler_params=pltpu.CompilerParams(vmem_limit_bytes=32 * 1024 * 1024),
@@ -336,28 +314,21 @@
 
     sent = jnp.concatenate([to_heads(latents), to_heads(new_span)], axis=1)
     sent = jnp.broadcast_to(sent[:, None], (heads, 2, 2 * rows, HEAD_DIM)).reshape(2 * heads, 2 * rows, HEAD_DIM)
-    got = lax.all_to_all(sent, "seq", 0, 0, tiled=True)
+    got = lax.all_to_all(sent, ("head", "half"), 0, 0, tiled=True)
     mine = got[:, :rows].reshape(SPAN, HEAD_DIM)
     fresh = got[:, rows:].reshape(SPAN, HEAD_DIM)
-    same = lax.all_gather(mine, "x", axis=0)
+    same = lax.all_to_all(jnp.broadcast_to(mine, (4, SPAN, HEAD_DIM)), "x", 0, 0, tiled=True)
     other = lax.ppermute(same, "core", [(0, 1), (1, 0)])
     done = both_steps(mesh_place, counts, steps, span_mask, delta, q_gain, k_gain, same, other, fresh)
-    back = lax.all_to_all(done, "seq", 0, 0, tiled=True)
-    back = back.reshape(heads, 2, 3 * rows, HEAD_DIM)
-
-    def to_tokens(block):
-        return block.transpose(1, 0, 2).reshape(rows, width)
-
-    part = back[:, :, rows : 2 * rows].astype(jnp.float32)
-    root = back[:, :, 2 * rows :].astype(jnp.float32)
-    ratio = root[:, 0] / root[:, 1]
-    share = 1.0 / (1.0 + ratio * ratio)
-    final = part[:, 0] + share * (part[:, 1] - part[:, 0])
-    return to_tokens(back[:, 0, :rows]), to_tokens(final.astype(jnp.bfloat16))
+    back = lax.all_to_all(done, "head", 0, 0, tiled=True)
+    return tuple(
+        back[:, k * rows : (k + 1) * rows].transpose(1, 0, 2).reshape(rows, width) for k in range(2)
+    )
 
 
 def solution(mesh):
-    mesh = Mesh(mesh.devices.reshape(4, 2, 64), ("x", "core", "seq"))
-    tokens = P(("x", "core", "seq"), None)
-    in_specs = (tokens, P("seq", None), P(), P(), P(), P(), P(), P())
+    mesh = Mesh(mesh.devices.reshape(4, 2, 32, 2), ("x", "core", "head", "half"))
+    seq = ("head", "half")
+    tokens = P(("x", "core", *seq), None)
+    in_specs = (tokens, P(seq, None), P(), P(), P(), P(), P(), P())
     return jax.shard_map(per_device, mesh=mesh, in_specs=in_specs, out_specs=(tokens, tokens), check_vma=False)

time: 82.6 us -> 78.7 us (0.953)
  blocking collectives: 64.9 us -> 58.8 us
  Pallas kernels: 10.4 us -> 13.1 us
    all_gather x1 -> x0, blocking collectives: 12.8 us -> none  [per_device(): same = lax.all_gather(mine, 'x', axis=0)]
    all_to_all x2 -> x3, blocking collectives: 52.1 us -> 58.8 us  [the longest x1 31.3 us: per_device(): got = lax.all_to_all(sent, ('head', 'half'), 0, 0, tiled=True)]
    pallas_call x1, Pallas kernels: 10.4 us -> 13.1 us  [both_steps(): pl.pallas_call(functools.partial(head_kernel, place), out_shape=jax.Shape...]
where the time goes in v3:
time: 78.7 us; the launch traced here: 78.3 us
  blocking collectives  58.8 us (75%)
  Pallas kernels  13.1 us (17%)
  starting transfers between devices  2.04 us (3%)
  waiting for transfers between devices  1.88 us (2%)
  other arithmetic  0.9 us (1%)
  local copies, waits for them, and re-layouts  0.81 us (1%)
    all_to_all x1, blocking collectives, per_device(): got = lax.all_to_all(sent, ('head', 'half'), 0, 0, tiled=True)  31.3 us
    all_to_all x1, blocking collectives, per_device(): back = lax.all_to_all(done, 'head', 0, 0, tiled=True)  16.8 us
    pallas_call x1, Pallas kernels, both_steps(): pl.pallas_call(functools.partial(head_kernel, place), out_shape=jax.Shape...  13.1 us
    all_to_all x1, blocking collectives, per_device(): lax.all_to_all(jnp.broadcast_to(mine, (4, SPAN, HEAD_DIM)), 'x', 0, 0, ti...  10.7 us
    ppermute x1, starting transfers between devices, per_device(): other = lax.ppermute(same, 'core', [(0, 1), (1, 0)])  2.04 us
    ppermute x1, waiting for transfers between devices, per_device(): other = lax.ppermute(same, 'core', [(0, 1), (1, 0)])  1.88 us
  transfers between devices with their start and end apart: 1, of which 1 were waited for; matrix products, arithmetic and copies ran while one was open for 0% of the time, Pallas kernels for 0%

profile of v3, /device:TPU:6, one launch (start us, length us, event | category | flops | bytes accessed | tf_op | source)
XLA Modules:
  0.0 78.3 jit_solution(16049173094522354035)
XLA Ops:
  0.6 0.9 %pad_maximum_fusion = bf16[32,16,128]{2,1,0:T(8,128)(2,1)S(1)} fusion(bf16[32,8,128]{2,1,0:T(8,128)(2,1)} %bitcast.20, bf16[32,8,128]{2,1,0:T(8,128)(2,1)} %bitcast.21), kind=kLoop, calls=%fused_computation.2 | loop fusion | flops 262144 | bytes 262144 | tf_op jit(solution)/shard_map/concatenate | solution.py:315
  1.6 31.3 %all_to_all.15 = bf16[64,16,128]{2,1,0:T(8,128)(2,1)S(1)} all-to-all(bf16[64,16,128]{2,1,0:T(8,128)(2,1)S(1)} %bitcast.19), channel_id=1, replica_groups=mesh['x'=4,'core'=2,'head'=32,'half'=2] {'head','half'}, dimensions={0} | all-to-all | bytes 524288 | tf_op jit(solution)/shard_map/all_to_all | solution.py:317
  32.9 0.0 copy-start
  32.9 0.0 copy-start.1
  32.9 0.1 broadcast_in_dim.10
  33.0 0.0 copy-start.2
  33.0 0.0 copy-start.5
  33.0 10.7 %all_to_all.16.same = bf16[4,512,128]{2,1,0:T(8,128)(2,1)S(1)} all-to-all(bf16[4,512,128]{2,1,0:T(8,128)(2,1)S(1)} %broadcast_in_dim.10), channel_id=1, replica_groups=mesh['x'=4,'core'=2,'head'=32,'half'=2] {'x'}, dimensions={0} | all-to-all | bytes 1048576 | tf_op jit(solution)/shard_map/all_to_all | solution.py:320
  43.7 0.0 copy-start.3
  43.7 0.0 copy-start.4
  43.7 2.0 %collective-permute-start = (bf16[4,512,128]{2,1,0:T(8,128)(2,1)S(1)}, bf16[4,512,128]{2,1,0:T(8,128)(2,1)S(1)}, u32[]{:S(2)}, u32[]{:S(2)}) collective-permute-start(bf16[4,512,128]{2,1,0:T(8,128)(2,1)S(1)} %all_to_all.16.same), channel_id=1, source_target_pairs={{0,64},{64,0},{1,65},{65,1},{2,66},{66,2},{3,67},{67,3},{4,68},{68... | collective-permute-start | bytes 1572872 | tf_op jit(solution)/shard_map/ppermute | solution.py:321
  45.8 1.9 %collective-permute-done.other = bf16[4,512,128]{2,1,0:T(8,128)(2,1)S(1)} collective-permute-done((bf16[4,512,128]{2,1,0:T(8,128)(2,1)S(1)}, bf16[4,512,128]{2,1,0:T(8,128)(2,1)S(1)}, u32[]{:S(2)}, u32[]{:S(2)}) %collective-permute-start) | collective-permute-done | bytes 524320 | tf_op jit(solution)/shard_map/ppermute | solution.py:321
  47.7 0.0 copy-done
  47.7 0.0 copy-done.1
  47.7 0.0 copy-done.2
  47.7 0.0 copy-done.5
  47.7 0.0 copy-done.3
  47.7 0.0 copy-done.4
  47.7 13.1 %shard_map.95 = bf16[32,16,128]{2,1,0:T(8,128)(2,1)S(1)} custom-call(s32[9]{0:T(128)S(1)} %copy-done.4, s32[2,8]{1,0:T(2,128)S(1)} %copy-done.3, s32[2,8,8]{2,1,0:T(8,128)S(1)} %copy-done.2, f32[64]{0:T(128)S(1)} %copy-done.5, f32[64,4096]{1,0:T(8,128)S(1)} %copy-done, f32[64,4096]{1,0:T(8,128)S(1)} %copy-done.1, bf16[4,512,128]{2,1,0:T(8,128)(2,1)S(1)} %all_to_all.16.same, ...), custom_call_target="tpu_custom_call" | custom-call | tf_op jit(solution)/shard_map/pallas_call | solution.py:280
  60.8 16.8 %all_to_all.17 = bf16[32,16,128]{2,1,0:T(8,128)(2,1)S(1)} all-to-all(bf16[32,16,128]{2,1,0:T(8,128)(2,1)S(1)} %shard_map.95), channel_id=1, replica_groups=mesh['x'=4,'core'=2,'head'=32,'half'=2] {'head'}, dimensions={0} | all-to-all | bytes 262144 | tf_op jit(solution)/shard_map/all_to_all | solution.py:323
  77.6 0.7 slice_bitcast_fusion.2
  (2 shorter events, 0.1 us)
Async XLA Ops:
  32.9 14.8 %copy-start = (f32[64,4096]{1,0:T(8,128)S(1)}, f32[64,4096]{1,0:T(8,128)}, u32[]{:S(2)}) copy-start(f32[64,4096]{1,0:T(8,128)} %q_gain.1) | copy-start | bytes 3145732
  32.9 14.8 %copy-start.1 = (f32[64,4096]{1,0:T(8,128)S(1)}, f32[64,4096]{1,0:T(8,128)}, u32[]{:S(2)}) copy-start(f32[64,4096]{1,0:T(8,128)} %k_gain.1) | copy-start | bytes 3145732
  33.0 14.7 %copy-start.2 = (s32[2,8,8]{2,1,0:T(8,128)S(1)}, s32[2,8,8]{2,1,0:T(8,128)}, u32[]{:S(2)}) copy-start(s32[2,8,8]{2,1,0:T(8,128)} %mask.1) | copy-start | bytes 1540
  33.0 14.7 %copy-start.5 = (f32[64]{0:T(128)S(1)}, f32[64]{0:T(128)}, u32[]{:S(2)}) copy-start(f32[64]{0:T(128)} %delta.1) | copy-start | bytes 772
  43.7 4.0 %copy-start.3 = (s32[2,8]{1,0:T(2,128)S(1)}, s32[2,8]{1,0:T(2,128)}, u32[]{:S(2)}) copy-start(s32[2,8]{1,0:T(2,128)} %steps.1) | copy-start | bytes 196
  43.7 4.0 %copy-start.4 = (s32[9]{0:T(128)S(1)}, s32[9]{0:T(128)}, u32[]{:S(2)}) copy-start(s32[9]{0:T(128)} %counts.1) | copy-start | bytes 112
  43.7 3.9 %collective-permute-start = (bf16[4,512,128]{2,1,0:T(8,128)(2,1)S(1)}, bf16[4,512,128]{2,1,0:T(8,128)(2,1)S(1)}, u32[]{:S(2)}, u32[]{:S(2)}) collective-permute-start(bf16[4,512,128]{2,1,0:T(8,128)(2,1)S(1)} %all_to_all.16.same), channel_id=1, source_target_pairs={{0,64},{64,0},{1,65},{65,1},{2,66},{66,2},{3,67},{67,3},{4,68},{68... | collective-permute-start | bytes 1572872 | tf_op jit(solution)/shard_map/ppermute | solution.py:321

commit v4 on v3

--- a/solution.py
+++ b/solution.py
@@ -16,7 +16,8 @@
 KEYS = 128
 PER_SPAN = SPAN // KEYS
 NONE = SPANS * PER_SPAN
-GROUP = 4
+FIRST = (4, 6, 8)
+REST = (2, 4, 8)
 ENTERING, MIDDLE, UNUSED = 0, 1, 2
 SCORE_SCALE = math.log2(math.e) / math.sqrt(HEAD_DIM)
 SHIFT = 40.0
@@ -116,7 +117,7 @@
             for r in range(PER_SPAN):
                 blocks[size + r] = PER_SPAN * i + r
             size += jnp.where(seen(i) > 0, (live(i) + KEYS - 1) // KEYS, 0)
-        for r in range(2 * GROUP):
+        for r in range(2 * FIRST[-1]):
             blocks[size + r] = NONE
         return size
 
@@ -139,22 +140,23 @@
             )
         return sum(parts[1:], parts[0])
 
-    def attend(q, rows, keys, values, size, slot):
-        acc[slot, :rows] = group(q, keys, values, 0, GROUP)
+    def attend(q, rows, keys, values, size, slot, pairs):
+        acc[slot, :rows] = group(q, keys, values, 0, pairs)
         if rows < SPAN:
             acc[slot, rows:] = jnp.ones((SPAN - rows, 2 * HEAD_DIM), jnp.float32)
-        rest = jnp.maximum((size + 1) // 2 - GROUP, 0)
-        whole = (rest + 1) // GROUP
-
-        def more(n, carry):
-            acc[slot, :rows] += group(q, keys, values, 2 * GROUP * (n + 1), GROUP)
-            return carry
-
-        lax.fori_loop(0, whole, more, 0)
-
-        @pl.when(rest > GROUP * whole)
-        def _():
-            acc[slot, :rows] += group(q, keys, values, 2 * GROUP * (whole + 1), GROUP // 2)
+        if pairs == FIRST[-1]:
+            rest = (size + 1) // 2 - pairs
+            for least_rest, more in zip((0, *REST), REST):
+
+                @pl.when(jnp.logical_and(rest > least_rest, rest <= more))
+                def _():
+                    acc[slot, :rows] += group(q, keys, values, 2 * pairs, more)
+
+    def by_size(size, step):
+        pairs = (size + 1) // 2
+        for fewer, most in zip((0, *FIRST), FIRST):
+            fits = pairs > fewer if most == FIRST[-1] else jnp.logical_and(pairs > fewer, pairs <= most)
+            pl.when(fits)(functools.partial(step, most))
 
     def attend_safe(q, rows, keys, values, size, live, slot):
         def scores(b):
@@ -216,16 +218,16 @@
         size = blocks_of(j)
         slot = lax.rem(m, 2)
 
-        def block(rows):
+        def block(rows, pairs):
             enter(before, 1 - slot, m > 0)
-            attend(query[j, :rows], rows, key, value, size, slot)
+            attend(query[j, :rows], rows, key, value, size, slot, pairs)
 
         rows = jnp.where(jnp.logical_or(j == g + 1, j == g), SPAN, counts[j])
         for r in range(2, PER_SPAN + 1):
             fits = rows <= r * KEYS
             if r > 2:
                 fits = jnp.logical_and(fits, rows > (r - 1) * KEYS)
-            pl.when(fits)(functools.partial(block, r * KEYS))
+            pl.when(fits)(lambda r=r: by_size(size, functools.partial(block, r * KEYS)))
         return carry
 
     lax.fori_loop(0, wanted, one, 0)
@@ -253,7 +255,7 @@
 
     size = list_blocks(lambda e: mask[1, g, e], lambda e: counts[e + 1])
     out[:, :8] = sent[MIDDLE].astype(jnp.bfloat16)
-    attend(query2[0], HALF, key2, value2, size, 0)
+    by_size(size, lambda pairs: attend(query2[0], HALF, key2, value2, size, 0, pairs))
 
     def put_final():
         x, total = finish(sent[ENTERING].reshape(HALF, HEAD_DIM), HALF, 0, delta[steps[1, g]])
@@ -295,7 +297,7 @@
             pltpu.VMEM((2, SPAN, 2 * HEAD_DIM), f32),
             pltpu.VMEM((SPAN, KEYS), f32),
             pltpu.VMEM((8, HEAD_DIM), f32),
-            pltpu.SMEM((NONE + 2 * GROUP,), jnp.int32),
+            pltpu.SMEM((NONE + 2 * FIRST[-1],), jnp.int32),
             pltpu.SMEM((SPANS + 2,), jnp.int32),
             pltpu.VMEM((UNUSED + 1, SPAN // 16, 8, HEAD_DIM), f32),
             pltpu.SemaphoreType.DMA((2,)),

time: 78.7 us -> 78.2 us (level)
  no operation moved by 1% of the time
where the time goes in v4:
time: 78.2 us; the launch traced here: 77.9 us
  blocking collectives  58.6 us (75%)
  Pallas kernels  13 us (17%)
  starting transfers between devices  2.04 us (3%)
  waiting for transfers between devices  1.88 us (2%)
  other arithmetic  0.9 us (1%)
  local copies, waits for them, and re-layouts  0.81 us (1%)
    all_to_all x1, blocking collectives, per_device(): got = lax.all_to_all(sent, ('head', 'half'), 0, 0, tiled=True)  31.3 us
    all_to_all x1, blocking collectives, per_device(): back = lax.all_to_all(done, 'head', 0, 0, tiled=True)  16.5 us
    pallas_call x1, Pallas kernels, both_steps(): pl.pallas_call(functools.partial(head_kernel, place), out_shape=jax.Shape...  13 us
    all_to_all x1, blocking collectives, per_device(): lax.all_to_all(jnp.broadcast_to(mine, (4, SPAN, HEAD_DIM)), 'x', 0, 0, ti...  10.7 us
    ppermute x1, starting transfers between devices, per_device(): other = lax.ppermute(same, 'core', [(0, 1), (1, 0)])  2.04 us
    ppermute x1, waiting for transfers between devices, per_device(): other = lax.ppermute(same, 'core', [(0, 1), (1, 0)])  1.88 us
  transfers between devices with their start and end apart: 1, of which 1 were waited for; matrix products, arithmetic and copies ran while one was open for 0% of the time, Pallas kernels for 0%

profile of v4, /device:TPU:6, one launch (start us, length us, event | category | flops | bytes accessed | tf_op | source)
XLA Modules:
  0.0 77.9 jit_solution(359523689229702174)
XLA Ops:
  0.6 0.9 %pad_maximum_fusion = bf16[32,16,128]{2,1,0:T(8,128)(2,1)S(1)} fusion(bf16[32,8,128]{2,1,0:T(8,128)(2,1)} %bitcast.20, bf16[32,8,128]{2,1,0:T(8,128)(2,1)} %bitcast.21), kind=kLoop, calls=%fused_computation.2 | loop fusion | flops 262144 | bytes 262144 | tf_op jit(solution)/shard_map/concatenate | solution.py:317
  1.6 31.3 %all_to_all.15 = bf16[64,16,128]{2,1,0:T(8,128)(2,1)S(1)} all-to-all(bf16[64,16,128]{2,1,0:T(8,128)(2,1)S(1)} %bitcast.19), channel_id=1, replica_groups=mesh['x'=4,'core'=2,'head'=32,'half'=2] {'head','half'}, dimensions={0} | all-to-all | bytes 524288 | tf_op jit(solution)/shard_map/all_to_all | solution.py:319
  32.9 0.0 copy-start
  32.9 0.0 copy-start.1
  32.9 0.1 broadcast_in_dim.10
  33.0 0.0 copy-start.2
  33.0 0.0 copy-start.5
  33.0 10.7 %all_to_all.16.same = bf16[4,512,128]{2,1,0:T(8,128)(2,1)S(1)} all-to-all(bf16[4,512,128]{2,1,0:T(8,128)(2,1)S(1)} %broadcast_in_dim.10), channel_id=1, replica_groups=mesh['x'=4,'core'=2,'head'=32,'half'=2] {'x'}, dimensions={0} | all-to-all | bytes 1048576 | tf_op jit(solution)/shard_map/all_to_all | solution.py:322
  43.7 0.0 copy-start.3
  43.7 0.0 copy-start.4
  43.7 2.0 %collective-permute-start = (bf16[4,512,128]{2,1,0:T(8,128)(2,1)S(1)}, bf16[4,512,128]{2,1,0:T(8,128)(2,1)S(1)}, u32[]{:S(2)}, u32[]{:S(2)}) collective-permute-start(bf16[4,512,128]{2,1,0:T(8,128)(2,1)S(1)} %all_to_all.16.same), channel_id=1, source_target_pairs={{0,64},{64,0},{1,65},{65,1},{2,66},{66,2},{3,67},{67,3},{4,68},{68... | collective-permute-start | bytes 1572872 | tf_op jit(solution)/shard_map/ppermute | solution.py:323
  45.8 1.9 %collective-permute-done.other = bf16[4,512,128]{2,1,0:T(8,128)(2,1)S(1)} collective-permute-done((bf16[4,512,128]{2,1,0:T(8,128)(2,1)S(1)}, bf16[4,512,128]{2,1,0:T(8,128)(2,1)S(1)}, u32[]{:S(2)}, u32[]{:S(2)}) %collective-permute-start) | collective-permute-done | bytes 524320 | tf_op jit(solution)/shard_map/ppermute | solution.py:323
  47.7 0.0 copy-done
  47.7 0.0 copy-done.1
  47.7 0.0 copy-done.2
  47.7 0.0 copy-done.5
  47.7 0.0 copy-done.3
  47.7 0.0 copy-done.4
  47.7 13.0 %shard_map.95 = bf16[32,16,128]{2,1,0:T(8,128)(2,1)S(1)} custom-call(s32[9]{0:T(128)S(1)} %copy-done.4, s32[2,8]{1,0:T(2,128)S(1)} %copy-done.3, s32[2,8,8]{2,1,0:T(8,128)S(1)} %copy-done.2, f32[64]{0:T(128)S(1)} %copy-done.5, f32[64,4096]{1,0:T(8,128)S(1)} %copy-done, f32[64,4096]{1,0:T(8,128)S(1)} %copy-done.1, bf16[4,512,128]{2,1,0:T(8,128)(2,1)S(1)} %all_to_all.16.same, ...), custom_call_target="tpu_custom_call" | custom-call | tf_op jit(solution)/shard_map/pallas_call | solution.py:282
  60.7 16.5 %all_to_all.17 = bf16[32,16,128]{2,1,0:T(8,128)(2,1)S(1)} all-to-all(bf16[32,16,128]{2,1,0:T(8,128)(2,1)S(1)} %shard_map.95), channel_id=1, replica_groups=mesh['x'=4,'core'=2,'head'=32,'half'=2] {'head'}, dimensions={0} | all-to-all | bytes 262144 | tf_op jit(solution)/shard_map/all_to_all | solution.py:325
  77.3 0.7 slice_bitcast_fusion.2
  (2 shorter events, 0.1 us)
Async XLA Ops:
  32.9 14.8 %copy-start = (f32[64,4096]{1,0:T(8,128)S(1)}, f32[64,4096]{1,0:T(8,128)}, u32[]{:S(2)}) copy-start(f32[64,4096]{1,0:T(8,128)} %q_gain.1) | copy-start | bytes 3145732
  32.9 14.8 %copy-start.1 = (f32[64,4096]{1,0:T(8,128)S(1)}, f32[64,4096]{1,0:T(8,128)}, u32[]{:S(2)}) copy-start(f32[64,4096]{1,0:T(8,128)} %k_gain.1) | copy-start | bytes 3145732
  33.0 14.7 %copy-start.2 = (s32[2,8,8]{2,1,0:T(8,128)S(1)}, s32[2,8,8]{2,1,0:T(8,128)}, u32[]{:S(2)}) copy-start(s32[2,8,8]{2,1,0:T(8,128)} %mask.1) | copy-start | bytes 1540
  33.0 14.7 %copy-start.5 = (f32[64]{0:T(128)S(1)}, f32[64]{0:T(128)}, u32[]{:S(2)}) copy-start(f32[64]{0:T(128)} %delta.1) | copy-start | bytes 772
  43.7 4.0 %copy-start.3 = (s32[2,8]{1,0:T(2,128)S(1)}, s32[2,8]{1,0:T(2,128)}, u32[]{:S(2)}) copy-start(s32[2,8]{1,0:T(2,128)} %steps.1) | copy-start | bytes 196
  43.7 4.0 %copy-start.4 = (s32[9]{0:T(128)S(1)}, s32[9]{0:T(128)}, u32[]{:S(2)}) copy-start(s32[9]{0:T(128)} %counts.1) | copy-start | bytes 112
  43.7 3.9 %collective-permute-start = (bf16[4,512,128]{2,1,0:T(8,128)(2,1)S(1)}, bf16[4,512,128]{2,1,0:T(8,128)(2,1)S(1)}, u32[]{:S(2)}, u32[]{:S(2)}) collective-permute-start(bf16[4,512,128]{2,1,0:T(8,128)(2,1)S(1)} %all_to_all.16.same), channel_id=1, source_target_pairs={{0,64},{64,0},{1,65},{65,1},{2,66},{66,2},{3,67},{67,3},{4,68},{68... | collective-permute-start | bytes 1572872 | tf_op jit(solution)/shard_map/ppermute | solution.py:323

commit v5 on v4

--- a/solution.py
+++ b/solution.py
@@ -185,8 +185,8 @@
         return (old + rate * (target - old)).astype(jnp.bfloat16), total
 
     def sent_rows(x):
-        pieces = x.astype(jnp.float32).reshape(SPAN // 16, 2, 8, HEAD_DIM)
-        return jnp.where(half == 0, pieces[:, 0], pieces[:, 1])
+        x = x.astype(jnp.float32)
+        return jnp.where(half == 0, x[:HALF], x[HALF:]).reshape(HALF // 8, 8, HEAD_DIM)
 
     def enter(j, slot, counted=True):
         x, total = finish(xs[j], SPAN, slot, delta[steps[0, j]])
@@ -315,8 +315,8 @@
         return block.reshape(rows, heads, HEAD_DIM).transpose(1, 0, 2)
 
     sent = jnp.concatenate([to_heads(latents), to_heads(new_span)], axis=1)
-    sent = jnp.broadcast_to(sent[:, None], (heads, 2, 2 * rows, HEAD_DIM)).reshape(2 * heads, 2 * rows, HEAD_DIM)
-    got = lax.all_to_all(sent, ("head", "half"), 0, 0, tiled=True)
+    sent = jnp.broadcast_to(sent, (2, heads, 2 * rows, HEAD_DIM)).reshape(2 * heads, 2 * rows, HEAD_DIM)
+    got = lax.all_to_all(sent, ("half", "head"), 0, 0, tiled=True)
     mine = got[:, :rows].reshape(SPAN, HEAD_DIM)
     fresh = got[:, rows:].reshape(SPAN, HEAD_DIM)
     same = lax.all_to_all(jnp.broadcast_to(mine, (4, SPAN, HEAD_DIM)), "x", 0, 0, tiled=True)
@@ -329,8 +329,8 @@
 
 
 def solution(mesh):
-    mesh = Mesh(mesh.devices.reshape(4, 2, 32, 2), ("x", "core", "head", "half"))
-    seq = ("head", "half")
+    mesh = Mesh(mesh.devices.reshape(4, 2, 2, 32), ("x", "core", "half", "head"))
+    seq = ("half", "head")
     tokens = P(("x", "core", *seq), None)
     in_specs = (tokens, P(seq, None), P(), P(), P(), P(), P(), P())
     return jax.shard_map(per_device, mesh=mesh, in_specs=in_specs, out_specs=(tokens, tokens), check_vma=False)

time: 78.2 us -> 76.1 us (0.973)
  blocking collectives: 58.6 us -> 56.7 us
  Pallas kernels: 13 us -> 12.1 us
    all_to_all x1, blocking collectives: 16.5 us -> 14.7 us  [per_device(): back = lax.all_to_all(done, 'head', 0, 0, tiled=True)]
    pallas_call x1, Pallas kernels: 13 us -> 12.1 us  [both_steps(): pl.pallas_call(functools.partial(head_kernel, place), out_shape=jax.Shape...]
where the time goes in v5:
time: 76.1 us; the launch traced here: 75.1 us
  blocking collectives  56.7 us (75%)
  Pallas kernels  12.1 us (16%)
  starting transfers between devices  2.04 us (3%)
  waiting for transfers between devices  1.88 us (2%)
  other arithmetic  0.9 us (1%)
  local copies, waits for them, and re-layouts  0.81 us (1%)
    all_to_all x1, blocking collectives, per_device(): got = lax.all_to_all(sent, ('half', 'head'), 0, 0, tiled=True)  31.3 us
    all_to_all x1, blocking collectives, per_device(): back = lax.all_to_all(done, 'head', 0, 0, tiled=True)  14.7 us
    pallas_call x1, Pallas kernels, both_steps(): pl.pallas_call(functools.partial(head_kernel, place), out_shape=jax.Shape...  12.1 us
    all_to_all x1, blocking collectives, per_device(): lax.all_to_all(jnp.broadcast_to(mine, (4, SPAN, HEAD_DIM)), 'x', 0, 0, ti...  10.7 us
    ppermute x1, starting transfers between devices, per_device(): other = lax.ppermute(same, 'core', [(0, 1), (1, 0)])  2.04 us
    ppermute x1, waiting for transfers between devices, per_device(): other = lax.ppermute(same, 'core', [(0, 1), (1, 0)])  1.88 us
  transfers between devices with their start and end apart: 1, of which 1 were waited for; matrix products, arithmetic and copies ran while one was open for 0% of the time, Pallas kernels for 0%

profile of v5, /device:TPU:6, one launch (start us, length us, event | category | flops | bytes accessed | tf_op | source)
XLA Modules:
  0.0 75.1 jit_solution(1313154461720051598)
XLA Ops:
  0.6 0.9 %pad_maximum_fusion = bf16[32,16,128]{2,1,0:T(8,128)(2,1)S(1)} fusion(bf16[32,8,128]{2,1,0:T(8,128)(2,1)} %bitcast.20, bf16[32,8,128]{2,1,0:T(8,128)(2,1)} %bitcast.21), kind=kLoop, calls=%fused_computation.2 | loop fusion | flops 262144 | bytes 262144 | tf_op jit(solution)/shard_map/concatenate | solution.py:317
  1.6 31.3 %all_to_all.15 = bf16[64,16,128]{2,1,0:T(8,128)(2,1)S(1)} all-to-all(bf16[64,16,128]{2,1,0:T(8,128)(2,1)S(1)} %bitcast.19), channel_id=1, replica_groups=mesh['x'=4,'core'=2,'half'=2,'head'=32] {'half','head'}, dimensions={0} | all-to-all | bytes 524288 | tf_op jit(solution)/shard_map/all_to_all | solution.py:319
  32.9 0.0 copy-start
  32.9 0.0 copy-start.1
  32.9 0.1 broadcast_in_dim.7
  33.0 0.0 copy-start.2
  33.0 0.0 copy-start.5
  33.0 10.7 %all_to_all.16.same = bf16[4,512,128]{2,1,0:T(8,128)(2,1)S(1)} all-to-all(bf16[4,512,128]{2,1,0:T(8,128)(2,1)S(1)} %broadcast_in_dim.7), channel_id=1, replica_groups=mesh['x'=4,'core'=2,'half'=2,'head'=32] {'x'}, dimensions={0} | all-to-all | bytes 1048576 | tf_op jit(solution)/shard_map/all_to_all | solution.py:322
  43.7 0.0 copy-start.3
  43.7 0.0 copy-start.4
  43.7 2.0 %collective-permute-start = (bf16[4,512,128]{2,1,0:T(8,128)(2,1)S(1)}, bf16[4,512,128]{2,1,0:T(8,128)(2,1)S(1)}, u32[]{:S(2)}, u32[]{:S(2)}) collective-permute-start(bf16[4,512,128]{2,1,0:T(8,128)(2,1)S(1)} %all_to_all.16.same), channel_id=1, source_target_pairs={{0,64},{64,0},{1,65},{65,1},{2,66},{66,2},{3,67},{67,3},{4,68},{68... | collective-permute-start | bytes 1572872 | tf_op jit(solution)/shard_map/ppermute | solution.py:323
  45.8 1.9 %collective-permute-done.other = bf16[4,512,128]{2,1,0:T(8,128)(2,1)S(1)} collective-permute-done((bf16[4,512,128]{2,1,0:T(8,128)(2,1)S(1)}, bf16[4,512,128]{2,1,0:T(8,128)(2,1)S(1)}, u32[]{:S(2)}, u32[]{:S(2)}) %collective-permute-start) | collective-permute-done | bytes 524320 | tf_op jit(solution)/shard_map/ppermute | solution.py:323
  47.7 0.0 copy-done
  47.7 0.0 copy-done.1
  47.7 0.0 copy-done.2
  47.7 0.0 copy-done.5
  47.7 0.0 copy-done.3
  47.7 0.0 copy-done.4
  47.7 12.1 %shard_map.95 = bf16[32,16,128]{2,1,0:T(8,128)(2,1)S(1)} custom-call(s32[9]{0:T(128)S(1)} %copy-done.4, s32[2,8]{1,0:T(2,128)S(1)} %copy-done.3, s32[2,8,8]{2,1,0:T(8,128)S(1)} %copy-done.2, f32[64]{0:T(128)S(1)} %copy-done.5, f32[64,4096]{1,0:T(8,128)S(1)} %copy-done, f32[64,4096]{1,0:T(8,128)S(1)} %copy-done.1, bf16[4,512,128]{2,1,0:T(8,128)(2,1)S(1)} %all_to_all.16.same, ...), custom_call_target="tpu_custom_call" | custom-call | tf_op jit(solution)/shard_map/pallas_call | solution.py:282
  59.8 14.7 %all_to_all.17 = bf16[32,16,128]{2,1,0:T(8,128)(2,1)S(1)} all-to-all(bf16[32,16,128]{2,1,0:T(8,128)(2,1)S(1)} %shard_map.95), channel_id=1, replica_groups=mesh['x'=4,'core'=2,'half'=2,'head'=32] {'head'}, dimensions={0} | all-to-all | bytes 262144 | tf_op jit(solution)/shard_map/all_to_all | solution.py:325
  74.5 0.7 slice_bitcast_fusion.2
  (2 shorter events, 0.1 us)
Async XLA Ops:
  32.9 14.8 %copy-start = (f32[64,4096]{1,0:T(8,128)S(1)}, f32[64,4096]{1,0:T(8,128)}, u32[]{:S(2)}) copy-start(f32[64,4096]{1,0:T(8,128)} %q_gain.1) | copy-start | bytes 3145732
  32.9 14.8 %copy-start.1 = (f32[64,4096]{1,0:T(8,128)S(1)}, f32[64,4096]{1,0:T(8,128)}, u32[]{:S(2)}) copy-start(f32[64,4096]{1,0:T(8,128)} %k_gain.1) | copy-start | bytes 3145732
  33.0 14.7 %copy-start.2 = (s32[2,8,8]{2,1,0:T(8,128)S(1)}, s32[2,8,8]{2,1,0:T(8,128)}, u32[]{:S(2)}) copy-start(s32[2,8,8]{2,1,0:T(8,128)} %mask.1) | copy-start | bytes 1540
  33.0 14.7 %copy-start.5 = (f32[64]{0:T(128)S(1)}, f32[64]{0:T(128)}, u32[]{:S(2)}) copy-start(f32[64]{0:T(128)} %delta.1) | copy-start | bytes 772
  43.7 4.0 %copy-start.3 = (s32[2,8]{1,0:T(2,128)S(1)}, s32[2,8]{1,0:T(2,128)}, u32[]{:S(2)}) copy-start(s32[2,8]{1,0:T(2,128)} %steps.1) | copy-start | bytes 196
  43.7 4.0 %copy-start.4 = (s32[9]{0:T(128)S(1)}, s32[9]{0:T(128)}, u32[]{:S(2)}) copy-start(s32[9]{0:T(128)} %counts.1) | copy-start | bytes 112
  43.7 3.9 %collective-permute-start = (bf16[4,512,128]{2,1,0:T(8,128)(2,1)S(1)}, bf16[4,512,128]{2,1,0:T(8,128)(2,1)S(1)}, u32[]{:S(2)}, u32[]{:S(2)}) collective-permute-start(bf16[4,512,128]{2,1,0:T(8,128)(2,1)S(1)} %all_to_all.16.same), channel_id=1, source_target_pairs={{0,64},{64,0},{1,65},{65,1},{2,66},{66,2},{3,67},{67,3},{4,68},{68... | collective-permute-start | bytes 1572872 | tf_op jit(solution)/shard_map/ppermute | solution.py:323

commit v6 on v5

--- a/solution.py
+++ b/solution.py
@@ -222,7 +222,8 @@
             enter(before, 1 - slot, m > 0)
             attend(query[j, :rows], rows, key, value, size, slot, pairs)
 
-        rows = jnp.where(jnp.logical_or(j == g + 1, j == g), SPAN, counts[j])
+        whole = jnp.logical_and(half == 1, jnp.logical_or(j == g + 1, j == g))
+        rows = jnp.where(whole, SPAN, counts[j])
         for r in range(2, PER_SPAN + 1):
             fits = rows <= r * KEYS
             if r > 2:

time: 76.1 us -> 74.1 us (0.974)
  Pallas kernels: 12.1 us -> 10.3 us
    pallas_call x1, Pallas kernels: 12.1 us -> 10.3 us  [both_steps(): pl.pallas_call(functools.partial(head_kernel, place), out_shape=jax.Shape...]
where the time goes in v6:
time: 74.1 us; the launch traced here: 73 us
  blocking collectives  56.4 us (76%)
  Pallas kernels  10.3 us (14%)
  starting transfers between devices  2.04 us (3%)
  waiting for transfers between devices  1.88 us (3%)
  other arithmetic  0.9 us (1%)
  local copies, waits for them, and re-layouts  0.81 us (1%)
    all_to_all x1, blocking collectives, per_device(): got = lax.all_to_all(sent, ('half', 'head'), 0, 0, tiled=True)  31.3 us
    all_to_all x1, blocking collectives, per_device(): back = lax.all_to_all(done, 'head', 0, 0, tiled=True)  14.4 us
    all_to_all x1, blocking collectives, per_device(): lax.all_to_all(jnp.broadcast_to(mine, (4, SPAN, HEAD_DIM)), 'x', 0, 0, ti...  10.7 us
    pallas_call x1, Pallas kernels, both_steps(): pl.pallas_call(functools.partial(head_kernel, place), out_shape=jax.Shape...  10.3 us
    ppermute x1, starting transfers between devices, per_device(): other = lax.ppermute(same, 'core', [(0, 1), (1, 0)])  2.04 us
    ppermute x1, waiting for transfers between devices, per_device(): other = lax.ppermute(same, 'core', [(0, 1), (1, 0)])  1.88 us
  transfers between devices with their start and end apart: 1, of which 1 were waited for; matrix products, arithmetic and copies ran while one was open for 0% of the time, Pallas kernels for 0%

profile of v6, /device:TPU:6, one launch (start us, length us, event | category | flops | bytes accessed | tf_op | source)
XLA Modules:
  0.0 73.0 jit_solution(8209924741225051265)
XLA Ops:
  0.6 0.9 %pad_maximum_fusion = bf16[32,16,128]{2,1,0:T(8,128)(2,1)S(1)} fusion(bf16[32,8,128]{2,1,0:T(8,128)(2,1)} %bitcast.20, bf16[32,8,128]{2,1,0:T(8,128)(2,1)} %bitcast.21), kind=kLoop, calls=%fused_computation.2 | loop fusion | flops 262144 | bytes 262144 | tf_op jit(solution)/shard_map/concatenate | solution.py:318
  1.6 31.3 %all_to_all.15 = bf16[64,16,128]{2,1,0:T(8,128)(2,1)S(1)} all-to-all(bf16[64,16,128]{2,1,0:T(8,128)(2,1)S(1)} %bitcast.19), channel_id=1, replica_groups=mesh['x'=4,'core'=2,'half'=2,'head'=32] {'half','head'}, dimensions={0} | all-to-all | bytes 524288 | tf_op jit(solution)/shard_map/all_to_all | solution.py:320
  32.9 0.0 copy-start
  32.9 0.0 copy-start.1
  32.9 0.1 broadcast_in_dim.7
  33.0 0.0 copy-start.2
  33.0 0.0 copy-start.5
  33.0 10.7 %all_to_all.16.same = bf16[4,512,128]{2,1,0:T(8,128)(2,1)S(1)} all-to-all(bf16[4,512,128]{2,1,0:T(8,128)(2,1)S(1)} %broadcast_in_dim.7), channel_id=1, replica_groups=mesh['x'=4,'core'=2,'half'=2,'head'=32] {'x'}, dimensions={0} | all-to-all | bytes 1048576 | tf_op jit(solution)/shard_map/all_to_all | solution.py:323
  43.7 0.0 copy-start.3
  43.7 0.0 copy-start.4
  43.7 2.0 %collective-permute-start = (bf16[4,512,128]{2,1,0:T(8,128)(2,1)S(1)}, bf16[4,512,128]{2,1,0:T(8,128)(2,1)S(1)}, u32[]{:S(2)}, u32[]{:S(2)}) collective-permute-start(bf16[4,512,128]{2,1,0:T(8,128)(2,1)S(1)} %all_to_all.16.same), channel_id=1, source_target_pairs={{0,64},{64,0},{1,65},{65,1},{2,66},{66,2},{3,67},{67,3},{4,68},{68... | collective-permute-start | bytes 1572872 | tf_op jit(solution)/shard_map/ppermute | solution.py:324
  45.8 1.9 %collective-permute-done.other = bf16[4,512,128]{2,1,0:T(8,128)(2,1)S(1)} collective-permute-done((bf16[4,512,128]{2,1,0:T(8,128)(2,1)S(1)}, bf16[4,512,128]{2,1,0:T(8,128)(2,1)S(1)}, u32[]{:S(2)}, u32[]{:S(2)}) %collective-permute-start) | collective-permute-done | bytes 524320 | tf_op jit(solution)/shard_map/ppermute | solution.py:324
  47.7 0.0 copy-done
  47.7 0.0 copy-done.1
  47.7 0.0 copy-done.2
  47.7 0.0 copy-done.5
  47.7 0.0 copy-done.3
  47.7 0.0 copy-done.4
  47.7 10.3 %shard_map.95 = bf16[32,16,128]{2,1,0:T(8,128)(2,1)S(1)} custom-call(s32[9]{0:T(128)S(1)} %copy-done.4, s32[2,8]{1,0:T(2,128)S(1)} %copy-done.3, s32[2,8,8]{2,1,0:T(8,128)S(1)} %copy-done.2, f32[64]{0:T(128)S(1)} %copy-done.5, f32[64,4096]{1,0:T(8,128)S(1)} %copy-done, f32[64,4096]{1,0:T(8,128)S(1)} %copy-done.1, bf16[4,512,128]{2,1,0:T(8,128)(2,1)S(1)} %all_to_all.16.same, ...), custom_call_target="tpu_custom_call" | custom-call | tf_op jit(solution)/shard_map/pallas_call | solution.py:283
  58.0 14.4 %all_to_all.17 = bf16[32,16,128]{2,1,0:T(8,128)(2,1)S(1)} all-to-all(bf16[32,16,128]{2,1,0:T(8,128)(2,1)S(1)} %shard_map.95), channel_id=1, replica_groups=mesh['x'=4,'core'=2,'half'=2,'head'=32] {'head'}, dimensions={0} | all-to-all | bytes 262144 | tf_op jit(solution)/shard_map/all_to_all | solution.py:326
  72.4 0.7 slice_bitcast_fusion.2
  (2 shorter events, 0.1 us)
Async XLA Ops:
  32.9 14.8 %copy-start = (f32[64,4096]{1,0:T(8,128)S(1)}, f32[64,4096]{1,0:T(8,128)}, u32[]{:S(2)}) copy-start(f32[64,4096]{1,0:T(8,128)} %q_gain.1) | copy-start | bytes 3145732
  32.9 14.8 %copy-start.1 = (f32[64,4096]{1,0:T(8,128)S(1)}, f32[64,4096]{1,0:T(8,128)}, u32[]{:S(2)}) copy-start(f32[64,4096]{1,0:T(8,128)} %k_gain.1) | copy-start | bytes 3145732
  33.0 14.7 %copy-start.2 = (s32[2,8,8]{2,1,0:T(8,128)S(1)}, s32[2,8,8]{2,1,0:T(8,128)}, u32[]{:S(2)}) copy-start(s32[2,8,8]{2,1,0:T(8,128)} %mask.1) | copy-start | bytes 1540
  33.0 14.7 %copy-start.5 = (f32[64]{0:T(128)S(1)}, f32[64]{0:T(128)}, u32[]{:S(2)}) copy-start(f32[64]{0:T(128)} %delta.1) | copy-start | bytes 772
  43.7 4.0 %copy-start.3 = (s32[2,8]{1,0:T(2,128)S(1)}, s32[2,8]{1,0:T(2,128)}, u32[]{:S(2)}) copy-start(s32[2,8]{1,0:T(2,128)} %steps.1) | copy-start | bytes 196
  43.7 4.0 %copy-start.4 = (s32[9]{0:T(128)S(1)}, s32[9]{0:T(128)}, u32[]{:S(2)}) copy-start(s32[9]{0:T(128)} %counts.1) | copy-start | bytes 112
  43.7 3.9 %collective-permute-start = (bf16[4,512,128]{2,1,0:T(8,128)(2,1)S(1)}, bf16[4,512,128]{2,1,0:T(8,128)(2,1)S(1)}, u32[]{:S(2)}, u32[]{:S(2)}) collective-permute-start(bf16[4,512,128]{2,1,0:T(8,128)(2,1)S(1)} %all_to_all.16.same), channel_id=1, source_target_pairs={{0,64},{64,0},{1,65},{65,1},{2,66},{66,2},{3,67},{67,3},{4,68},{68... | collective-permute-start | bytes 1572872 | tf_op jit(solution)/shard_map/ppermute | solution.py:324
